TPU v7x, 128 devices: a whole 4x4x4 slice. The times are simulated.
128 devices in a mesh: bank: 32 (over x, y, core), dp: 4 (over z).
Axes of the slice: x: 4, y: 4, z: 4, core: 2. Of those that a mesh axis runs over, the one named last changes fastest.
Arguments:
- clips: bfloat16 [8192, 256], P(('bank', 'dp')), may hold values from -1 to 1
- queue: bfloat16 [262144, 256], P('bank'), may hold values from -8 to 8
- positive: int32 [8192], P(('bank', 'dp')), may hold values from 0 to 262143, as said below
- cotangent: float32 [8192], P(('bank', 'dp')), may hold values from 0.5 to 12
Outputs:
- clip_grads: float32 [8192, 256], P(('bank', 'dp'))
Inputs may be any that keep to these rules, and one draw needn't show every extreme that they name: The clips form 262144 // 8192 equal consecutive groups; the positive of a clip of group g lies among entries g * 8192 to (g + 1) * 8192 - 1.
All inputs are finite; a program needn't handle non-finite values.
Results may differ from a plain program's by a relative error of at most 0.00055.
Values may be sent and summed in bfloat16 or wider, within the bound.
A program may use at most 64 MiB of HBM per device.

v0:
```python
import math

import jax
import jax.numpy as jnp
from jax import lax
from jax.sharding import PartitionSpec as P

logit_sharpness = 1.0 / 0.07
epsilon = 1e-06
clip_scale = 4.0


def inverse_norms(values):
    return lax.rsqrt(jnp.sum(values * values, axis=1) + epsilon)


def sweep(unit_rows, queue):
    queue_entry_count = queue.shape[0]
    block_width = min(1024, queue_entry_count)
    stacked = queue.reshape(queue_entry_count // block_width, block_width, queue.shape[1])
    row_total = unit_rows.shape[0]

    def advance(carry, queue_block):
        totals, moments = carry
        reciprocal = inverse_norms(queue_block.astype(jnp.float32))
        similarity_logits = lax.dot_general(
            unit_rows, queue_block, (((1,), (1,)), ((), ())), preferred_element_type=jnp.float32
        )
        logit_power = jnp.exp(similarity_logits * (reciprocal * logit_sharpness)[None, :])
        totals = totals + jnp.sum(logit_power, axis=1)
        weights = (logit_power * reciprocal[None, :]).astype(jnp.bfloat16)
        moments = moments + jnp.dot(weights, queue_block, preferred_element_type=jnp.float32)
        return ((totals, moments), None)

    start_carry = (
        jnp.zeros((row_total,), jnp.float32),
        jnp.zeros((row_total, queue.shape[1]), jnp.float32),
    )
    result, unused = lax.scan(advance, start_carry, stacked)
    return result


def shards(clips, queue, positive, cotangent):
    own_raw = clips.astype(jnp.float32)
    own_inverse = inverse_norms(own_raw)
    own_dirs = own_raw * own_inverse[:, None]
    unit_rows = lax.all_gather(own_dirs.astype(jnp.bfloat16), "bank", axis=0, tiled=True)
    own_count = clips.shape[0]
    partial_totals, moments = sweep(unit_rows, queue)
    own_moments, own_totals = (
        lax.psum_scatter(moments, "bank", scatter_dimension=0, tiled=True),
        lax.psum_scatter(partial_totals, "bank", scatter_dimension=0, tiled=True),
    )
    quotient = own_moments / own_totals[:, None]
    local_index = positive - lax.axis_index("bank") * queue.shape[0]
    positive_rows = jnp.take(queue, local_index, axis=0).astype(jnp.float32)
    pushed = quotient - inverse_norms(positive_rows)[:, None] * positive_rows
    tangent = pushed - own_dirs * jnp.sum(own_dirs * pushed, axis=1, keepdims=True)
    gradient = cotangent[:, None] * tangent * own_inverse[:, None]
    squares = lax.psum(jnp.sum(gradient * gradient), ("bank", "dp"))
    clip_total = own_count * lax.axis_size("bank") * lax.axis_size("dp")
    ceiling = clip_scale * math.sqrt(clip_total)
    factor = jnp.minimum(1.0, ceiling / jnp.sqrt(squares + epsilon))
    return gradient * factor


def solution(mesh):
    in_specs = (P(("bank", "dp"), None), P("bank", None), P(("bank", "dp")), P(("bank", "dp")))
    out_specs = P(("bank", "dp"), None)
    return jax.shard_map(shards, mesh=mesh, in_specs=in_specs, out_specs=out_specs, check_vma=False)
```

profile of v0, /device:TPU:1, one launch (start us, length us, event | category | flops | bytes accessed | tf_op | source)
XLA Modules:
  0.0 317.1 jit_solution(11610910369301479813)
XLA Ops:
  6.5 0.0 all-gather.2.cloned.1.call-start
  6.5 0.9 fusion.19
  7.4 1.5 fusion.14
  8.9 0.0 all-gather.2.cloned.1.call-update
  8.9 0.0 reduce-scatter.2.cloned.1.call-start
  9.0 47.0 %all-gather.2.cloned.1.call-done = bf16[2048,256]{1,0:T(8,128)(2,1)} async-done(((bf16[64,256]{1,0:T(8,128)(2,1)}), bf16[2048,256]{1,0:T(8,128)(2,1)}) %all-gather.2.cloned.1.call-update) | async-done | bytes 1048592 | tf_op jit(solution)/shard_map/all_gather | solution.py:47
  55.9 0.0 copy-start.3
  55.9 0.0 copy-start.4
  55.9 0.0 copy-start.1
  55.9 0.0 copy-start.2
  56.0 107.4 %while.13 = (s32[]{:T(128)}, f32[2048]{0:T(1024)S(1)}, f32[2048,256]{1,0:T(8,128)S(1)}, bf16[8,1024,256]{2,1,0:T(8,128)(2,1)}, bf16[2048,256]{1,0:T(8,128)(2,1)}, /*index=5*/s32[]{:T(128)}, s32[]{:T(128)}) while((s32[]{:T(128)}, f32[2048]{0:T(1024)S(1)}, f32[2048,256]{1,0:T(8,128)S(1)}, bf16[8,1024,256]{2,1,0:T(8,128)(2,1)}, ...), condition=%wide.region_4.5_spmd.clone, body=%wide.region_1.4_spmd.clone.sunk | while | flops 2159807488 | bytes 23655516 | solution.py:39
  56.0 1.3 multiply_reduce_fusion.3
  57.3 5.9 %fusion.30 = (f32[2048]{0:T(1024)S(1)}, f32[1024,2048]{1,0:T(8,128)}) fusion(f32[1024]{0:T(1024)S(1)} %get-tuple-element.106, bf16[2048,256]{1,0:T(8,128)(2,1)} %get-tuple-element.128, bf16[8,1024,256]{2,1,0:T(8,128)(2,1)} %get-tuple-element.127, s32[]{:T(128)} %get-tuple-element.117), kind=kOutput, calls=%fused_computation.3.clone.1 | convolution fusion | flops 1077934080 | bytes 9974272 | tf_op jit(solution)/shard_map/while/body/eval_jaxpr/dot_general | solution.py:26
  63.2 6.2 %fusion.31 = f32[2048,256]{1,0:T(8,128)S(1)} fusion(f32[1024,2048]{1,0:T(8,128)} %get-tuple-element.108, f32[1024]{0:T(1024)S(1)} %get-tuple-element.109, f32[1024]{0:T(1024)S(1)} %get-tuple-element.106, f32[2048,256]{1,0:T(8,128)S(1)} %get-tuple-element.119, pred[]{:T(512)S(6)} %compare.3, bf16[8,1024,256]{2,1,0:T(8,128)(2,1)} %get-tuple-element.127, ...), kind=kOutput, calls=%fused_computation.7.clone.1 | convolution fusion | flops 1081081856 | bytes 13115905 | tf_op jit(solution)/shard_map/while/body/eval_jaxpr/dot_general | solution.py:32
  69.4 1.3 multiply_reduce_fusion.3
  70.7 5.9 %fusion.30 = (f32[2048]{0:T(1024)S(1)}, f32[1024,2048]{1,0:T(8,128)}) fusion(f32[1024]{0:T(1024)S(1)} %get-tuple-element.106, bf16[2048,256]{1,0:T(8,128)(2,1)} %get-tuple-element.128, bf16[8,1024,256]{2,1,0:T(8,128)(2,1)} %get-tuple-element.127, s32[]{:T(128)} %get-tuple-element.117), kind=kOutput, calls=%fused_computation.3.clone.1 | convolution fusion | flops 1077934080 | bytes 9974272 | tf_op jit(solution)/shard_map/while/body/eval_jaxpr/dot_general | solution.py:26
  76.6 6.2 %fusion.31 = f32[2048,256]{1,0:T(8,128)S(1)} fusion(f32[1024,2048]{1,0:T(8,128)} %get-tuple-element.108, f32[1024]{0:T(1024)S(1)} %get-tuple-element.109, f32[1024]{0:T(1024)S(1)} %get-tuple-element.106, f32[2048,256]{1,0:T(8,128)S(1)} %get-tuple-element.119, pred[]{:T(512)S(6)} %compare.3, bf16[8,1024,256]{2,1,0:T(8,128)(2,1)} %get-tuple-element.127, ...), kind=kOutput, calls=%fused_computation.7.clone.1 | convolution fusion | flops 1081081856 | bytes 13115905 | tf_op jit(solution)/shard_map/while/body/eval_jaxpr/dot_general | solution.py:32
  82.8 1.3 multiply_reduce_fusion.3
  84.1 5.9 %fusion.30 = (f32[2048]{0:T(1024)S(1)}, f32[1024,2048]{1,0:T(8,128)}) fusion(f32[1024]{0:T(1024)S(1)} %get-tuple-element.106, bf16[2048,256]{1,0:T(8,128)(2,1)} %get-tuple-element.128, bf16[8,1024,256]{2,1,0:T(8,128)(2,1)} %get-tuple-element.127, s32[]{:T(128)} %get-tuple-element.117), kind=kOutput, calls=%fused_computation.3.clone.1 | convolution fusion | flops 1077934080 | bytes 9974272 | tf_op jit(solution)/shard_map/while/body/eval_jaxpr/dot_general | solution.py:26
  90.1 6.2 %fusion.31 = f32[2048,256]{1,0:T(8,128)S(1)} fusion(f32[1024,2048]{1,0:T(8,128)} %get-tuple-element.108, f32[1024]{0:T(1024)S(1)} %get-tuple-element.109, f32[1024]{0:T(1024)S(1)} %get-tuple-element.106, f32[2048,256]{1,0:T(8,128)S(1)} %get-tuple-element.119, pred[]{:T(512)S(6)} %compare.3, bf16[8,1024,256]{2,1,0:T(8,128)(2,1)} %get-tuple-element.127, ...), kind=kOutput, calls=%fused_computation.7.clone.1 | convolution fusion | flops 1081081856 | bytes 13115905 | tf_op jit(solution)/shard_map/while/body/eval_jaxpr/dot_general | solution.py:32
  96.3 1.3 multiply_reduce_fusion.3
  97.6 5.9 %fusion.30 = (f32[2048]{0:T(1024)S(1)}, f32[1024,2048]{1,0:T(8,128)}) fusion(f32[1024]{0:T(1024)S(1)} %get-tuple-element.106, bf16[2048,256]{1,0:T(8,128)(2,1)} %get-tuple-element.128, bf16[8,1024,256]{2,1,0:T(8,128)(2,1)} %get-tuple-element.127, s32[]{:T(128)} %get-tuple-element.117), kind=kOutput, calls=%fused_computation.3.clone.1 | convolution fusion | flops 1077934080 | bytes 9974272 | tf_op jit(solution)/shard_map/while/body/eval_jaxpr/dot_general | solution.py:26
  103.5 6.2 %fusion.31 = f32[2048,256]{1,0:T(8,128)S(1)} fusion(f32[1024,2048]{1,0:T(8,128)} %get-tuple-element.108, f32[1024]{0:T(1024)S(1)} %get-tuple-element.109, f32[1024]{0:T(1024)S(1)} %get-tuple-element.106, f32[2048,256]{1,0:T(8,128)S(1)} %get-tuple-element.119, pred[]{:T(512)S(6)} %compare.3, bf16[8,1024,256]{2,1,0:T(8,128)(2,1)} %get-tuple-element.127, ...), kind=kOutput, calls=%fused_computation.7.clone.1 | convolution fusion | flops 1081081856 | bytes 13115905 | tf_op jit(solution)/shard_map/while/body/eval_jaxpr/dot_general | solution.py:32
  109.7 1.3 multiply_reduce_fusion.3
  111.0 5.9 %fusion.30 = (f32[2048]{0:T(1024)S(1)}, f32[1024,2048]{1,0:T(8,128)}) fusion(f32[1024]{0:T(1024)S(1)} %get-tuple-element.106, bf16[2048,256]{1,0:T(8,128)(2,1)} %get-tuple-element.128, bf16[8,1024,256]{2,1,0:T(8,128)(2,1)} %get-tuple-element.127, s32[]{:T(128)} %get-tuple-element.117), kind=kOutput, calls=%fused_computation.3.clone.1 | convolution fusion | flops 1077934080 | bytes 9974272 | tf_op jit(solution)/shard_map/while/body/eval_jaxpr/dot_general | solution.py:26
  116.9 6.2 %fusion.31 = f32[2048,256]{1,0:T(8,128)S(1)} fusion(f32[1024,2048]{1,0:T(8,128)} %get-tuple-element.108, f32[1024]{0:T(1024)S(1)} %get-tuple-element.109, f32[1024]{0:T(1024)S(1)} %get-tuple-element.106, f32[2048,256]{1,0:T(8,128)S(1)} %get-tuple-element.119, pred[]{:T(512)S(6)} %compare.3, bf16[8,1024,256]{2,1,0:T(8,128)(2,1)} %get-tuple-element.127, ...), kind=kOutput, calls=%fused_computation.7.clone.1 | convolution fusion | flops 1081081856 | bytes 13115905 | tf_op jit(solution)/shard_map/while/body/eval_jaxpr/dot_general | solution.py:32
  123.1 1.3 multiply_reduce_fusion.3
  124.4 5.9 %fusion.30 = (f32[2048]{0:T(1024)S(1)}, f32[1024,2048]{1,0:T(8,128)}) fusion(f32[1024]{0:T(1024)S(1)} %get-tuple-element.106, bf16[2048,256]{1,0:T(8,128)(2,1)} %get-tuple-element.128, bf16[8,1024,256]{2,1,0:T(8,128)(2,1)} %get-tuple-element.127, s32[]{:T(128)} %get-tuple-element.117), kind=kOutput, calls=%fused_computation.3.clone.1 | convolution fusion | flops 1077934080 | bytes 9974272 | tf_op jit(solution)/shard_map/while/body/eval_jaxpr/dot_general | solution.py:26
  130.3 6.2 %fusion.31 = f32[2048,256]{1,0:T(8,128)S(1)} fusion(f32[1024,2048]{1,0:T(8,128)} %get-tuple-element.108, f32[1024]{0:T(1024)S(1)} %get-tuple-element.109, f32[1024]{0:T(1024)S(1)} %get-tuple-element.106, f32[2048,256]{1,0:T(8,128)S(1)} %get-tuple-element.119, pred[]{:T(512)S(6)} %compare.3, bf16[8,1024,256]{2,1,0:T(8,128)(2,1)} %get-tuple-element.127, ...), kind=kOutput, calls=%fused_computation.7.clone.1 | convolution fusion | flops 1081081856 | bytes 13115905 | tf_op jit(solution)/shard_map/while/body/eval_jaxpr/dot_general | solution.py:32
  136.6 1.3 multiply_reduce_fusion.3
  137.8 5.9 %fusion.30 = (f32[2048]{0:T(1024)S(1)}, f32[1024,2048]{1,0:T(8,128)}) fusion(f32[1024]{0:T(1024)S(1)} %get-tuple-element.106, bf16[2048,256]{1,0:T(8,128)(2,1)} %get-tuple-element.128, bf16[8,1024,256]{2,1,0:T(8,128)(2,1)} %get-tuple-element.127, s32[]{:T(128)} %get-tuple-element.117), kind=kOutput, calls=%fused_computation.3.clone.1 | convolution fusion | flops 1077934080 | bytes 9974272 | tf_op jit(solution)/shard_map/while/body/eval_jaxpr/dot_general | solution.py:26
  143.8 6.2 %fusion.31 = f32[2048,256]{1,0:T(8,128)S(1)} fusion(f32[1024,2048]{1,0:T(8,128)} %get-tuple-element.108, f32[1024]{0:T(1024)S(1)} %get-tuple-element.109, f32[1024]{0:T(1024)S(1)} %get-tuple-element.106, f32[2048,256]{1,0:T(8,128)S(1)} %get-tuple-element.119, pred[]{:T(512)S(6)} %compare.3, bf16[8,1024,256]{2,1,0:T(8,128)(2,1)} %get-tuple-element.127, ...), kind=kOutput, calls=%fused_computation.7.clone.1 | convolution fusion | flops 1081081856 | bytes 13115905 | tf_op jit(solution)/shard_map/while/body/eval_jaxpr/dot_general | solution.py:32
  150.0 1.3 multiply_reduce_fusion.3
  151.3 5.9 %fusion.30 = (f32[2048]{0:T(1024)S(1)}, f32[1024,2048]{1,0:T(8,128)}) fusion(f32[1024]{0:T(1024)S(1)} %get-tuple-element.106, bf16[2048,256]{1,0:T(8,128)(2,1)} %get-tuple-element.128, bf16[8,1024,256]{2,1,0:T(8,128)(2,1)} %get-tuple-element.127, s32[]{:T(128)} %get-tuple-element.117), kind=kOutput, calls=%fused_computation.3.clone.1 | convolution fusion | flops 1077934080 | bytes 9974272 | tf_op jit(solution)/shard_map/while/body/eval_jaxpr/dot_general | solution.py:26
  157.2 6.2 %fusion.31 = f32[2048,256]{1,0:T(8,128)S(1)} fusion(f32[1024,2048]{1,0:T(8,128)} %get-tuple-element.108, f32[1024]{0:T(1024)S(1)} %get-tuple-element.109, f32[1024]{0:T(1024)S(1)} %get-tuple-element.106, f32[2048,256]{1,0:T(8,128)S(1)} %get-tuple-element.119, pred[]{:T(512)S(6)} %compare.3, bf16[8,1024,256]{2,1,0:T(8,128)(2,1)} %get-tuple-element.127, ...), kind=kOutput, calls=%fused_computation.7.clone.1 | convolution fusion | flops 1081081856 | bytes 13115905 | tf_op jit(solution)/shard_map/while/body/eval_jaxpr/dot_general | solution.py:32
  163.4 0.0 copy-start
  163.4 1.3 copy-done
  164.8 0.0 reduce-scatter.2.cloned.1.call-update
  164.8 0.0 copy-done.3
  164.8 3.4 %gather_fusion = bf16[64,256]{1,0:T(8,128)(2,1)S(1)} fusion(bf16[8192,256]{1,0:T(8,128)(2,1)} %bitcast.20, s32[1024]{0:T(1024)S(1)} %pad_clamp_fusion), kind=kCustom, calls=%fused_computation | custom fusion | bytes 65792 | tf_op jit(solution)/shard_map/jit(_take)/gather | solution.py:56
  168.2 0.0 copy-done.4
  168.2 0.6 dynamic-slice
  169.5 0.2 fusion.20
  169.7 63.4 %all-reduce = f32[2048]{0:T(1024)S(1)} all-reduce(f32[2048]{0:T(1024)S(1)} %get-tuple-element.34), channel_id=3, replica_groups=mesh['bank'=32,'dp'=4] {'bank'}, use_global_device_ids=true, to_apply=%region_6.7.clone | all-reduce | flops 2048 | bytes 16384
  233.1 0.1 dynamic-slice.1
  233.1 7.8 %reduce-scatter.2.cloned.1.call-done = f32[64,256]{1,0:T(8,128)} async-done(((f32[2048,256]{1,0:T(8,128)}), f32[64,256]{1,0:T(8,128)}) %reduce-scatter.2.cloned.1.call-update) | async-done | bytes 65552 | tf_op jit(solution)/shard_map/reduce_scatter | solution.py:51
  241.0 0.0 copy-done.1
  241.0 1.0 fusion.15
  242.0 0.0 copy-done.2
  242.0 0.7 multiply_reduce_fusion.1
  242.7 66.1 %psum.7 = f32[]{:T(128)} all-reduce(f32[]{:T(128)} %multiply_reduce_fusion.1), channel_id=1, replica_groups=mesh['bank'=32,'dp'=4] {'bank','dp'}, use_global_device_ids=true, to_apply=%region_10.11 | all-reduce | flops 1 | bytes 8 | tf_op jit(solution)/shard_map/psum | solution.py:60
  309.5 0.7 broadcast_multiply_fusion.1
  (22 shorter events, 0.1 us)
Async XLA Ops:
  6.5 49.4 %all-gather.2.cloned.1.call-start = ((), (), s32[]{:S(2)}) async-start(), calls=%async_computation.1 | async-start | bytes 1081344 | tf_op jit(solution)/shard_map/all_gather | solution.py:47
  8.9 232.1 %reduce-scatter.2.cloned.1.call-start = ((), (), s32[]{:S(2)}) async-start(), calls=%async_computation.2 | async-start | bytes 2162688 | tf_op jit(solution)/shard_map/reduce_scatter | solution.py:51
  55.9 108.9 %copy-start.3 = (s32[64]{0:T(128)S(1)}, s32[64]{0:T(128)}, u32[]{:S(2)}) copy-start(s32[64]{0:T(128)} %param.8) | copy-start | bytes 772
  55.9 112.3 %copy-start.4 = (u32[128]{0:T(128)S(1)}, u32[128]{0:T(128)}, u32[]{:S(2)}) copy-start(u32[128]{0:T(128)} %constant.53) | copy-start | bytes 1540
  55.9 185.0 %copy-start.1 = (bf16[64,256]{1,0:T(8,128)(2,1)S(1)}, bf16[64,256]{1,0:T(8,128)(2,1)}, u32[]{:S(2)}) copy-start(bf16[64,256]{1,0:T(8,128)(2,1)} %param.6) | copy-start | bytes 98308
  55.9 186.1 %copy-start.2 = (f32[64]{0:T(128)S(1)}, f32[64]{0:T(128)}, u32[]{:S(2)}) copy-start(f32[64]{0:T(128)} %param.9) | copy-start | bytes 772
  163.4 1.4 copy-start
Sparse Core Ops, SparseCore 0:
  9.6 46.2 all-gather.1
  164.9 76.0 reduce-scatter.1
where the time goes:
time: 318 us; the launch traced here: 317 us
  blocking collectives  129 us (41%)
  matrix products  96.9 us (30%)
  waiting for transfers between devices  54.8 us (17%)
  other arithmetic  15.2 us (5%)
  between operations  14.9 us (5%)
  local copies, waits for them, and re-layouts  5.41 us (2%)
    psum x1, blocking collectives, shards(): squares = lax.psum(jnp.sum(gradient * gradient), ('bank', 'dp'))  66.1 us
    unnamed x1, blocking collectives  63.4 us
    dot_general x8, matrix products, advance(): jnp.dot(weights, queue_block, preferred_element_type=jnp.float32)  49.4 us
    dot_general x8, matrix products, advance(): lax.dot_general(unit_rows, queue_block, (((1,), (1,)), ((), ())), preferr...  47.5 us
    all_gather x1, waiting for transfers between devices, shards(): lax.all_gather(own_dirs.astype(jnp.bfloat16), 'bank', axis=0, tiled=True)  47 us
    reduce_sum x10, other arithmetic, inverse_norms(): return lax.rsqrt(jnp.sum(values * values, axis=1) + epsilon)  11.1 us
    reduce_scatter x1, waiting for transfers between devices, shards(): lax.psum_scatter(moments, 'bank', scatter_dimension=0, tiled=True)  7.81 us
  transfers between devices with their start and end apart: 2, of which 2 were waited for; matrix products, arithmetic and copies ran while one was open for 1% of the time, Pallas kernels for 0%

commit v1 on v0

v1 whole, which is shorter than its diff:
```python
import math

import jax
import jax.numpy as jnp
from jax import lax
from jax.experimental import pallas as pl
from jax.experimental.pallas import tpu as pltpu
from jax.sharding import PartitionSpec as P

MESH = pl.DeviceIdType.MESH
LOG2E = 1.4426950408889634
SHARP = 1.0 / 0.07
EPS = 1e-6
F32 = jnp.float32
BF16 = jnp.bfloat16

OWN = 64
D = 256
KQ = 8192
CH = 512
PC = OWN + 8
KB = 2048
SK = 512
STEPS = KQ // KB
NCH = 4
PARTS = 4


def inverse_norms(v):
    return lax.rsqrt(jnp.sum(v * v, axis=1, keepdims=True) + EPS)


def kernel(clips_ref, queue_hbm, pos_ref, cot_ref, out_ref,
           q_ref, rec_ref, sc_ref, rows, acc, tacc, mbuf, pbuf, sbuf, abuf, lbuf, bbuf, prow, sq,
           qsem, gs, gr, ps, pr, ms, mr, as_, ar, bs, br, ss, sr):
    bank = lax.axis_index("bank")
    z = lax.axis_index("dp")
    c = lax.rem(bank, 2)
    y = lax.rem(bank // 2, 4)
    x = bank // 8
    a = (1 - c) * y + c * x
    b = (1 - c) * x + c * y
    step_a = 2 + 6 * c
    step_b = 8 - 6 * c
    partner = bank + 1 - 2 * c

    def dev_a(j):
        return (bank + (lax.rem(a + j, 4) - a) * step_a, z)

    def dev_b(j):
        return (bank + (lax.rem(b + j, 4) - b) * step_b, z)

    def remote(src, dst, s, r, dev):
        return pltpu.make_async_remote_copy(
            src_ref=src, dst_ref=dst, send_sem=s, recv_sem=r, device_id=dev, device_id_type=MESH)

    def queue_copy(i):
        part = pl.ds(i * (KQ // PARTS), KQ // PARTS)
        return pltpu.make_async_copy(queue_hbm.at[part], q_ref.at[part], qsem.at[i])

    for i in range(PARTS):
        queue_copy(i).start()

    barrier = pltpu.get_barrier_semaphore()
    peers = [dev_a(j) for j in (1, 2, 3)] + [dev_b(j) for j in (1, 2, 3)]
    far = []
    for dc in range(2):
        for dz in range(4):
            if dc or dz:
                far.append((bank + dc * (1 - 2 * c), lax.rem(z + dz, 4)))
    for dev in peers + far:
        pl.semaphore_signal(barrier, inc=1, device_id=dev, device_id_type=MESH)

    raw = clips_ref[...].astype(F32)
    inv = inverse_norms(raw)
    dirs = raw * inv
    own0 = pl.multiple_of(c * 256, 256)
    rows[0, pl.ds(own0, OWN), :] = dirs.astype(BF16)

    pl.semaphore_wait(barrier, len(peers) + len(far))

    def piece(t, j, n=1):
        return rows.at[t, pl.ds(pl.multiple_of(own0 + j * OWN, OWN), n * OWN)]

    def a_row(t, j):
        return remote(piece(t, 0), piece(t, j), gs.at[t * 4 + j], gr.at[t * 4 + j], dev_a(4 - j))

    def b_row(t):
        return remote(piece(0, 0), piece(t, 0), gs.at[t * 4], gr.at[t * 4], dev_b(4 - t))

    def p_row(t, j, n, i):
        return remote(piece(t, j, n), piece(t, j, n), ps.at[i], pr.at[i], (partner, z))

    def p_wait(t, j, n, i):
        other = rows.at[t, pl.ds(pl.multiple_of((1 - c) * 256 + j * OWN, OWN), n * OWN)]
        remote(other, other, ps.at[i], pr.at[i], (partner, z)).wait_recv()

    for j in (1, 2, 3):
        a_row(0, j).start()
    p_row(0, 0, 1, 4).start()
    for t in (1, 2, 3):
        b_row(t).start()

    eye = lax.broadcasted_iota(jnp.int32, (OWN, OWN), 0) == lax.broadcasted_iota(jnp.int32, (OWN, OWN), 1)
    local = (pos_ref[...] - bank * KQ).astype(F32).reshape(1, OWN)
    local_col = jnp.sum(jnp.where(eye, local, 0.0), axis=1, keepdims=True).astype(jnp.int32)
    prow[...] = jnp.zeros_like(prow)
    ones = jnp.ones((8, D), BF16)

    def prep(k0, n):
        qb = q_ref[pl.ds(k0, n), :]
        qf = qb.astype(F32)
        s2 = qf * qf
        hi = s2.astype(BF16)
        lo = (s2 - hi.astype(F32)).astype(BF16)
        dims = (((1,), (1,)), ((), ()))
        tot = lax.dot_general(ones, hi, dims, preferred_element_type=F32)
        tot = tot + lax.dot_general(ones, lo, dims, preferred_element_type=F32)
        r = lax.rsqrt(tot[0:1, :] + EPS)
        rec_ref[:, pl.ds(k0, n)] = r
        sc_ref[:, pl.ds(k0, n)] = r * (LOG2E * SHARP)
        place = lax.broadcasted_iota(jnp.int32, (OWN, n), 1) + k0
        hot = jnp.where(place == local_col, 1.0, 0.0).astype(BF16)
        prow[...] += jnp.dot(hot, qb, preferred_element_type=F32)

    for i in range(PARTS):
        queue_copy(i).wait()
        size = KQ // PARTS

        def prep_step(k, _, i=i):
            prep(pl.multiple_of(i * size + k * 512, 512), 512)
            return 0

        lax.fori_loop(0, size // 512, prep_step, 0)

    for j in (1, 2, 3):
        a_row(0, j).wait_recv()
    p_row(0, 1, 3, 0).start()
    for t in (1, 2, 3):
        b_row(t).wait_recv()
        for j in (1, 2, 3):
            a_row(t, j).start()
    p_wait(0, 0, 1, 4)
    p_wait(0, 1, 3, 0)

    half = 4 * PC
    mine0 = pl.multiple_of(c * half, half)
    theirs0 = pl.multiple_of((1 - c) * half, half)

    def to_partner(t):
        return remote(mbuf.at[t, pl.ds(theirs0, half)], pbuf.at[t], ms.at[t], mr.at[t], (partner, z))

    def a_sum(t, j):
        return remote(sbuf.at[t, pl.ds(j * PC, PC)], abuf.at[t, pl.ds((j - 1) * PC, PC)],
                      as_.at[t * 4 + j], ar.at[t * 4 + j], dev_a(j))

    def b_sum(t):
        return remote(lbuf.at[t], bbuf.at[t], bs.at[t], br.at[t], dev_b(t))

    def finish_chunk(t):
        for cc in range(2):
            for j in range(4):
                src = (cc * 4 + j) * OWN
                dst = cc * half + j * PC
                mbuf[t, dst:dst + OWN, :] = acc[src:src + OWN, :]
                col = jnp.sum(tacc[src:src + OWN, :], axis=1, keepdims=True)
                row = jnp.sum(jnp.where(eye, col, 0.0), axis=0, keepdims=True)
                mbuf[t, dst + OWN:dst + PC, :] = jnp.zeros((8, D), F32)
                mbuf[t, dst + OWN:dst + PC, 0:OWN] = jnp.broadcast_to(row, (8, OWN))
        to_partner(t).start()

    def level2(t):
        to_partner(t).wait_recv()
        sbuf[t] = mbuf[t, pl.ds(mine0, half), :] + pbuf[t]
        for j in (1, 2, 3):
            a_sum(t, j).start()

    def level3(t):
        for j in (1, 2, 3):
            a_sum(t, j).wait_recv()
        lbuf[t] = (sbuf[t, 0:PC, :] + abuf[t, 0:PC, :]) + (abuf[t, PC:2 * PC, :] + abuf[t, 2 * PC:3 * PC, :])

        @pl.when(t > 0)
        def _():
            b_sum(t).start()

    def compute(t, s):
        k0 = pl.multiple_of(s * KB, KB)
        total = tacc[...]
        rb = rows[t]
        weights = []
        for i in range(KB // SK):
            k = pl.ds(k0 + i * SK, SK)
            logits = lax.dot_general(rb, q_ref[k, :], (((1,), (1,)), ((), ())), preferred_element_type=F32)
            e = jnp.exp2(logits * sc_ref[:, k])
            for l in range(SK // 128):
                total = total + e[:, l * 128:(l + 1) * 128]
            weights.append((e * rec_ref[:, k]).astype(BF16))
        tacc[...] = total
        acc[...] += jnp.dot(jnp.concatenate(weights, axis=1), q_ref[pl.ds(k0, KB), :], preferred_element_type=F32)

    def step(n, _):
        t = n // STEPS
        s = lax.rem(n, STEPS)

        @pl.when(s == 0)
        def _():
            acc[...] = jnp.zeros_like(acc)
            tacc[...] = jnp.zeros_like(tacc)

            @pl.when(t > 0)
            def _():
                p_wait(t, 0, 4, t)

        compute(t, s)

        @pl.when(n == 1)
        def _():
            for t2 in (1, 2, 3):
                for j in (1, 2, 3):
                    a_row(t2, j).wait_recv()
                p_row(t2, 0, 4, t2).start()

        @pl.when((s == 0) & (t > 0))
        def _():
            level2(t - 1)

        @pl.when((s == 2) & (t > 0))
        def _():
            level3(t - 1)

        @pl.when(s == STEPS - 1)
        def _():
            finish_chunk(t)

        return 0

    lax.fori_loop(0, NCH * STEPS, step, 0)
    level2(NCH - 1)
    prows = prow[...]
    pushed_away = inverse_norms(prows) * prows
    level3(NCH - 1)
    own = lbuf[0]
    for t in (1, 2, 3):
        b_sum(t).wait_recv()
        own = own + bbuf[t]
    totals = jnp.sum(jnp.where(eye, own[OWN:OWN + 1, 0:OWN], 0.0), axis=1, keepdims=True)
    pushed = own[0:OWN, :] / totals - pushed_away
    tangent = pushed - dirs * jnp.sum(dirs * pushed, axis=1, keepdims=True)
    cot = jnp.sum(jnp.where(eye, cot_ref[...].reshape(1, OWN), 0.0), axis=1, keepdims=True)
    gradient = cot * tangent * inv

    squares = jnp.broadcast_to(jnp.sum(gradient * gradient, keepdims=True).reshape(1, 1), (8, 128))

    def round_trip(value, first, devices):
        sq[first] = value
        copies = []
        for i, dev in enumerate(devices):
            n = first + 1 + i
            copies.append(remote(sq.at[first], sq.at[n], ss.at[n], sr.at[n], dev))
            copies[-1].start()
        for i, copy in enumerate(copies):
            copy.wait_recv()
            value = value + sq[first + 1 + i]
        return value, copies

    squares, c1 = round_trip(squares, 0, peers[0:3])
    squares, c2 = round_trip(squares, 4, peers[3:6])
    squares, c3 = round_trip(squares, 8, far)
    clip_total = OWN * lax.axis_size("bank") * lax.axis_size("dp")
    factor = jnp.minimum(1.0, (4.0 * math.sqrt(clip_total)) / jnp.sqrt(squares[0:1, 0:1] + EPS))
    out_ref[...] = gradient * factor

    for copy in c1 + c2 + c3:
        copy.wait_send()
    for t in range(4):
        for j in (1, 2, 3):
            a_row(t, j).wait_send()
            a_sum(t, j).wait_send()
        to_partner(t).wait_send()
        if t:
            b_row(t).wait_send()
            b_sum(t).wait_send()
            p_row(t, 0, 4, t).wait_send()
    p_row(0, 0, 1, 4).wait_send()
    p_row(0, 1, 3, 0).wait_send()


def shards(clips, queue, positive, cotangent):
    vmem = pl.BlockSpec(memory_space=pltpu.VMEM)
    dma = pltpu.SemaphoreType.DMA
    return pl.pallas_call(
        kernel,
        out_shape=jax.ShapeDtypeStruct((OWN, D), F32),
        in_specs=[vmem, pl.BlockSpec(memory_space=pl.ANY), vmem, vmem],
        out_specs=vmem,
        scratch_shapes=[
            pltpu.VMEM((KQ, D), BF16),
            pltpu.VMEM((1, KQ), F32),
            pltpu.VMEM((1, KQ), F32),
            pltpu.VMEM((NCH, CH, D), BF16),
            pltpu.VMEM((CH, D), F32),
            pltpu.VMEM((CH, 128), F32),
            pltpu.VMEM((NCH, 8 * PC, D), F32),
            pltpu.VMEM((NCH, 4 * PC, D), F32),
            pltpu.VMEM((NCH, 4 * PC, D), F32),
            pltpu.VMEM((NCH, 3 * PC, D), F32),
            pltpu.VMEM((NCH, PC, D), F32),
            pltpu.VMEM((NCH, PC, D), F32),
            pltpu.VMEM((OWN, D), F32),
            pltpu.VMEM((16, 8, 128), F32),
            dma((PARTS,)),
            dma((16,)), dma((16,)),
            dma((5,)), dma((5,)),
            dma((4,)), dma((4,)),
            dma((16,)), dma((16,)),
            dma((4,)), dma((4,)),
            dma((16,)), dma((16,)),
        ],
        compiler_params=pltpu.CompilerParams(
            collective_id=0, has_side_effects=True, vmem_limit_bytes=56 << 20),
        cost_estimate=pl.CostEstimate(flops=17 * 10**9, bytes_accessed=5 * 10**6, transcendentals=17 * 10**6),
    )(clips, queue, positive, cotangent)


def solution(mesh):
    in_specs = (P(("bank", "dp"), None), P("bank", None), P(("bank", "dp")), P(("bank", "dp")))
    return jax.shard_map(shards, mesh=mesh, in_specs=in_specs, out_specs=P(("bank", "dp"), None), check_vma=False)
```

time: 318 us -> 69.6 us (0.22)
  blocking collectives: 129 us -> 0 us
  matrix products: 96.9 us -> 0 us
  Pallas kernels: 0 us -> 67.9 us
  waiting for transfers between devices: 54.8 us -> 0 us
  other arithmetic: 15.2 us -> 0 us
  between operations: 14.9 us -> 0.01 us
  local copies, waits for them, and re-layouts: 5.41 us -> 1.47 us
    dot_general x16 -> x0, matrix products: 96.9 us -> none  [the longest x8 49.4 us: advance(): jnp.dot(weights, queue_block, preferred_element_type=jnp.float32)]
    pallas_call x0 -> x1, Pallas kernels: none -> 67.9 us  [shards(): pl.pallas_call(kernel, out_shape=jax.ShapeDtypeStruct((OWN, D), F32), in_...]
    psum x1 -> x0, blocking collectives: 66.1 us -> none  [shards(): squares = lax.psum(jnp.sum(gradient * gradient), ('bank', 'dp'))]
    unnamed x1 -> x0, blocking collectives: 63.4 us -> none
    all_gather x1 -> x0, waiting for transfers between devices: 47 us -> none  [shards(): lax.all_gather(own_dirs.astype(jnp.bfloat16), 'bank', axis=0, tiled=True)]
    reduce_sum x12 -> x0, other arithmetic: 12.9 us -> none  [the longest x10 11.1 us: inverse_norms(): return lax.rsqrt(jnp.sum(values * values, axis=1) + epsilon)]
    reduce_scatter x1 -> x0, waiting for transfers between devices: 7.81 us -> none  [shards(): lax.psum_scatter(moments, 'bank', scatter_dimension=0, tiled=True)]
    gather x1 -> x0, local copies, waits for them, and re-layouts: 3.38 us -> none  [shards(): positive_rows = jnp.take(queue, local_index, axis=0).astype(jnp.float32)]
  transfers between devices with their start and end apart: 2 -> 0, of which waited for: 2 -> 0; matrix products, arithmetic and copies ran while one was open for 1% -> 0% of each run, Pallas kernels for 0% -> 0%
where the time goes in v1:
time: 69.6 us; the launch traced here: 69.4 us
  Pallas kernels  67.9 us (98%)
  local copies, waits for them, and re-layouts  1.47 us (2%)
    pallas_call x1, Pallas kernels, shards(): pl.pallas_call(kernel, out_shape=jax.ShapeDtypeStruct((OWN, D), F32), in_...  67.9 us
    unnamed x1, local copies, waits for them, and re-layouts  1.47 us

profile of v1, /device:TPU:1, one launch (start us, length us, event | category | flops | bytes accessed | tf_op | source)
XLA Modules:
  0.0 69.4 jit_solution(7188877845537362079)
XLA Ops:
  0.0 67.9 %shard_map.46 = f32[64,256]{1,0:T(8,128)} custom-call(bf16[64,256]{1,0:T(8,128)(2,1)} %clips_ref.1, bf16[8192,256]{1,0:T(8,128)(2,1)} %queue_hbm.1, s32[64]{0:T(128)} %pos_ref.1, f32[64]{0:T(128)} %cot_ref.1), custom_call_target="tpu_custom_call" | custom-call | flops 16999999488 | bytes 5000000 | tf_op jit(solution)/shard_map/pallas_call | solution.py:292
  67.9 1.5 %copy.6 = f32[64,256]{1,0:T(8,128)} copy(f32[64,256]{1,0:T(8,128)} %shard_map.46) | data formatting | bytes 131072

commit v2 on v1

v2 whole, which is shorter than its diff:
```python
import math

import jax
import jax.numpy as jnp
from jax import lax
from jax.experimental import pallas as pl
from jax.experimental.pallas import tpu as pltpu
from jax.sharding import PartitionSpec as P

MESH = pl.DeviceIdType.MESH
LOG2E = 1.4426950408889634
SHARP = 1.0 / 0.07
EPS = 1e-6
F32 = jnp.float32
BF16 = jnp.bfloat16

OWN = 64
D = 256
KQ = 8192
CH = 512
PC = OWN + 8
KB = 2048
SK = 512
STEPS = KQ // KB
NCH = 4
PARTS = 4


def inverse_norms(v):
    return lax.rsqrt(jnp.sum(v * v, axis=1, keepdims=True) + EPS)


def hops(o):
    return sum(min(v, 4 - v) for v in (o[0] % 4, o[1] % 4, o[3] % 4))


CHUNKS = (
    ((0, 0), (1, 1), (1, 3), (3, 1)),
    ((3, 3), (2, 0), (0, 2), (2, 2)),
    ((2, 1), (2, 3), (1, 2), (3, 2)),
    ((1, 0), (3, 0), (0, 1), (0, 3)),
)
NEAR = [(dx, dy, 0, 0) for dx in (0, 1, 3) for dy in (0, 1, 3) if dx or dy]
COLUMN = [(0, 0, dc, dz) for dc in range(2) for dz in range(4) if dc or dz]
ALL = sorted(
    [(dx, dy, dc, dz) for dx in range(4) for dy in range(4) for dc in range(2) for dz in range(4) if dx or dy or dc or dz],
    key=lambda o: -hops(o))


def kernel(clips_ref, queue_hbm, pos_ref, cot_ref, out_ref,
           q_ref, rec_ref, sc_ref, rows, acc, tacc, mbuf, pbuf, sbuf, abuf, prow, sq,
           qsem, go_near, go_column, gs, gr, ps, pr, ms, mr, as_, ar, ss, sr):
    bank = lax.axis_index("bank")
    z = lax.axis_index("dp")
    c = lax.rem(bank, 2)
    y = lax.rem(bank // 2, 4)
    x = bank // 8

    def device(o):
        dx, dy, dc, dz = o
        bx = lax.rem(x + dx, 4) if dx else x
        by = lax.rem(y + dy, 4) if dy else y
        bc = 1 - c if dc else c
        return ((bx * 4 + by) * 2 + bc, lax.rem(z + dz, 4) if dz else z)

    def chip(t, j, back=False):
        dx, dy = CHUNKS[t][j]
        return device(((4 - dx) % 4, (4 - dy) % 4, 0, 0) if back else (dx, dy, 0, 0))

    def remote(src, dst, s, r, dev):
        return pltpu.make_async_remote_copy(
            src_ref=src, dst_ref=dst, send_sem=s, recv_sem=r, device_id=dev, device_id_type=MESH)

    def queue_copy(i):
        part = pl.ds(i * (KQ // PARTS), KQ // PARTS)
        return pltpu.make_async_copy(queue_hbm.at[part], q_ref.at[part], qsem.at[i])

    barrier = pltpu.get_barrier_semaphore()
    for o in NEAR + COLUMN:
        pl.semaphore_signal(barrier, inc=1, device_id=device(o), device_id_type=MESH)
    for i in range(PARTS):
        queue_copy(i).start()

    raw = clips_ref[...].astype(F32)
    inv = inverse_norms(raw)
    dirs = raw * inv
    own0 = pl.multiple_of(c * 256, 256)
    rows[0, pl.ds(own0, OWN), :] = dirs.astype(BF16)

    pl.semaphore_wait(barrier, len(NEAR) + len(COLUMN))

    def piece(t, j, n=1):
        return rows.at[t, pl.ds(pl.multiple_of(own0 + j * OWN, OWN), n * OWN)]

    def row_copy(t, j):
        return remote(piece(0, 0), piece(t, j), gs.at[t * 4 + j], gr.at[t * 4 + j], chip(t, j, back=True))

    def relay(t, j, n, i):
        return remote(piece(t, j, n), piece(t, j, n), ps.at[i], pr.at[i], device((0, 0, 1, 0)))

    def relay_wait(t, j, n, i):
        other = rows.at[t, pl.ds(pl.multiple_of((1 - c) * 256 + j * OWN, OWN), n * OWN)]
        remote(other, other, ps.at[i], pr.at[i], device((0, 0, 1, 0))).wait_recv()

    for j in (1, 2, 3):
        row_copy(0, j).start()
    relay(0, 0, 1, 4).start()
    for o in NEAR:
        pl.semaphore_signal(go_near, inc=1, device_id=device(o), device_id_type=MESH)

    eye = lax.broadcasted_iota(jnp.int32, (OWN, OWN), 0) == lax.broadcasted_iota(jnp.int32, (OWN, OWN), 1)
    local = (pos_ref[...] - bank * KQ).astype(F32).reshape(1, OWN)
    local_col = jnp.sum(jnp.where(eye, local, 0.0), axis=1, keepdims=True).astype(jnp.int32)
    prow[...] = jnp.zeros_like(prow)
    ones = jnp.ones((8, D), BF16)

    def prep(k0, n):
        qb = q_ref[pl.ds(k0, n), :]
        qf = qb.astype(F32)
        s2 = qf * qf
        hi = s2.astype(BF16)
        lo = (s2 - hi.astype(F32)).astype(BF16)
        dims = (((1,), (1,)), ((), ()))
        tot = lax.dot_general(ones, hi, dims, preferred_element_type=F32)
        tot = tot + lax.dot_general(ones, lo, dims, preferred_element_type=F32)
        r = lax.rsqrt(tot[0:1, :] + EPS)
        rec_ref[:, pl.ds(k0, n)] = r
        sc_ref[:, pl.ds(k0, n)] = r * (LOG2E * SHARP)
        place = lax.broadcasted_iota(jnp.int32, (OWN, n), 1) + k0
        hot = jnp.where(place == local_col, 1.0, 0.0).astype(BF16)
        prow[...] += jnp.dot(hot, qb, preferred_element_type=F32)

    def prep_part(i):
        queue_copy(i).wait()
        size = KQ // PARTS

        def prep_step(k, _):
            prep(pl.multiple_of(i * size + k * 512, 512), 512)
            return 0

        lax.fori_loop(0, size // 512, prep_step, 0)

    for i in range(PARTS):
        prep_part(i)

    pl.semaphore_wait(go_near, len(NEAR))
    for t in (1, 2, 3):
        for j in range(4):
            row_copy(t, j).start()
    for o in COLUMN:
        pl.semaphore_signal(go_column, inc=1, device_id=device(o), device_id_type=MESH)

    for j in (1, 2, 3):
        row_copy(0, j).wait_recv()
    relay(0, 1, 3, 0).start()
    relay_wait(0, 0, 1, 4)
    relay_wait(0, 1, 3, 0)

    half = 4 * PC
    mine0 = pl.multiple_of(c * half, half)
    theirs0 = pl.multiple_of((1 - c) * half, half)

    def to_partner(t):
        return remote(mbuf.at[t, pl.ds(theirs0, half)], pbuf.at[t], ms.at[t], mr.at[t], device((0, 0, 1, 0)))

    def to_owner(t, j):
        i = t * 4 + j
        return remote(sbuf.at[t, pl.ds(j * PC, PC)], abuf.at[i], as_.at[i], ar.at[i], chip(t, j))

    def finish_chunk(t):
        for cc in range(2):
            for j in range(4):
                src = (cc * 4 + j) * OWN
                dst = cc * half + j * PC
                mbuf[t, dst:dst + OWN, :] = acc[src:src + OWN, :]
                col = jnp.sum(tacc[src:src + OWN, :], axis=1, keepdims=True)
                row = jnp.sum(jnp.where(eye, col, 0.0), axis=0, keepdims=True)
                mbuf[t, dst + OWN:dst + PC, :] = jnp.zeros((8, D), F32)
                mbuf[t, dst + OWN:dst + PC, 0:OWN] = jnp.broadcast_to(row, (8, OWN))
        to_partner(t).start()

    def send_sums(t):
        to_partner(t).wait_recv()
        sbuf[t] = mbuf[t, pl.ds(mine0, half), :] + pbuf[t]
        for j in range(4):
            if t or j:
                to_owner(t, j).start()

    def compute(t, s):
        k0 = pl.multiple_of(s * KB, KB)
        total = tacc[...]
        rb = rows[t]
        weights = []
        for i in range(KB // SK):
            k = pl.ds(k0 + i * SK, SK)
            logits = lax.dot_general(rb, q_ref[k, :], (((1,), (1,)), ((), ())), preferred_element_type=F32)
            e = jnp.exp2(logits * sc_ref[:, k])
            for l in range(SK // 128):
                total = total + e[:, l * 128:(l + 1) * 128]
            weights.append((e * rec_ref[:, k]).astype(BF16))
        tacc[...] = total
        acc[...] += jnp.dot(jnp.concatenate(weights, axis=1), q_ref[pl.ds(k0, KB), :], preferred_element_type=F32)

    def step(n, _):
        t = n // STEPS
        s = lax.rem(n, STEPS)

        @pl.when(s == 0)
        def _():
            acc[...] = jnp.zeros_like(acc)
            tacc[...] = jnp.zeros_like(tacc)

            @pl.when(t > 0)
            def _():
                relay_wait(t, 0, 4, t)

        compute(t, s)

        for t2, after in ((1, 2), (2, 3), (3, 4)):
            @pl.when(n == after)
            def _(t2=t2):
                for j in range(4):
                    row_copy(t2, j).wait_recv()
                relay(t2, 0, 4, t2).start()

        for t2 in range(NCH - 1):
            @pl.when(n == (t2 + 1) * STEPS)
            def _(t2=t2):
                send_sums(t2)

        @pl.when(s == STEPS - 1)
        def _():
            finish_chunk(t)

        return 0

    lax.fori_loop(0, NCH * STEPS, step, 0)
    send_sums(NCH - 1)
    pl.semaphore_wait(go_column, len(COLUMN))
    prows = prow[...]
    pushed_away = inverse_norms(prows) * prows
    cot = jnp.sum(jnp.where(eye, cot_ref[...].reshape(1, OWN), 0.0), axis=1, keepdims=True)
    own = sbuf[0, 0:PC, :]
    for i in range(1, 16):
        to_owner(i // 4, i % 4).wait_recv()
        own = own + abuf[i]
    totals = jnp.sum(jnp.where(eye, own[OWN:OWN + 1, 0:OWN], 0.0), axis=1, keepdims=True)
    pushed = own[0:OWN, :] / totals - pushed_away
    tangent = pushed - dirs * jnp.sum(dirs * pushed, axis=1, keepdims=True)
    gradient = cot * tangent * inv

    squares = jnp.sum(gradient * gradient, axis=0, keepdims=True)
    sq[0] = squares[:, 0:128] + squares[:, 128:256]
    for i, o in enumerate(ALL):
        remote(sq.at[0], sq.at[i + 1], ss, sr, device(o)).start()
    others = sq.at[pl.ds(1, len(ALL))]
    remote(others, others, ss, sr, device((0, 0, 1, 0))).wait()
    squares = jnp.sum(jnp.sum(sq[...], axis=0), axis=1, keepdims=True)
    clip_total = OWN * lax.axis_size("bank") * lax.axis_size("dp")
    factor = jnp.minimum(1.0, (4.0 * math.sqrt(clip_total)) / jnp.sqrt(squares + EPS))
    out_ref[...] = gradient * factor

    for t in range(4):
        to_partner(t).wait_send()
        for j in range(4):
            if t or j:
                row_copy(t, j).wait_send()
                to_owner(t, j).wait_send()
        if t:
            relay(t, 0, 4, t).wait_send()
    relay(0, 0, 1, 4).wait_send()
    relay(0, 1, 3, 0).wait_send()


def shards(clips, queue, positive, cotangent):
    vmem = pl.BlockSpec(memory_space=pltpu.VMEM)
    dma = pltpu.SemaphoreType.DMA
    return pl.pallas_call(
        kernel,
        out_shape=jax.ShapeDtypeStruct((OWN, D), F32),
        in_specs=[vmem, pl.BlockSpec(memory_space=pl.ANY), vmem, vmem],
        out_specs=vmem,
        scratch_shapes=[
            pltpu.VMEM((KQ, D), BF16),
            pltpu.VMEM((1, KQ), F32),
            pltpu.VMEM((1, KQ), F32),
            pltpu.VMEM((NCH, CH, D), BF16),
            pltpu.VMEM((CH, D), F32),
            pltpu.VMEM((CH, 128), F32),
            pltpu.VMEM((NCH, 8 * PC, D), F32),
            pltpu.VMEM((NCH, 4 * PC, D), F32),
            pltpu.VMEM((NCH, 4 * PC, D), F32),
            pltpu.VMEM((16, PC, D), F32),
            pltpu.VMEM((OWN, D), F32),
            pltpu.VMEM((len(ALL) + 1, 1, 128), F32),
            dma((PARTS,)),
            pltpu.SemaphoreType.REGULAR, pltpu.SemaphoreType.REGULAR,
            dma((16,)), dma((16,)),
            dma((5,)), dma((5,)),
            dma((4,)), dma((4,)),
            dma((16,)), dma((16,)),
            dma, dma,
        ],
        compiler_params=pltpu.CompilerParams(
            collective_id=0, has_side_effects=True, vmem_limit_bytes=56 << 20),
        cost_estimate=pl.CostEstimate(flops=17 * 10**9, bytes_accessed=5 * 10**6, transcendentals=17 * 10**6),
    )(clips, queue, positive, cotangent)


def solution(mesh):
    in_specs = (P(("bank", "dp"), None), P("bank", None), P(("bank", "dp")), P(("bank", "dp")))
    return jax.shard_map(shards, mesh=mesh, in_specs=in_specs, out_specs=P(("bank", "dp"), None), check_vma=False)
```

time: 69.6 us -> 56.5 us (0.81)
  Pallas kernels: 67.9 us -> 54.8 us
    pallas_call x1, Pallas kernels: 67.9 us -> 54.8 us  [shards(): pl.pallas_call(kernel, out_shape=jax.ShapeDtypeStruct((OWN, D), F32), in_...]
where the time goes in v2:
time: 56.5 us; the launch traced here: 56.3 us
  Pallas kernels  54.8 us (97%)
  local copies, waits for them, and re-layouts  1.47 us (3%)
    pallas_call x1, Pallas kernels, shards(): pl.pallas_call(kernel, out_shape=jax.ShapeDtypeStruct((OWN, D), F32), in_...  54.8 us
    unnamed x1, local copies, waits for them, and re-layouts  1.47 us

profile of v2, /device:TPU:1, one launch (start us, length us, event | category | flops | bytes accessed | tf_op | source)
XLA Modules:
  0.0 56.3 jit_solution(4041540965518476070)
XLA Ops:
  0.0 54.8 %shard_map.46 = f32[64,256]{1,0:T(8,128)} custom-call(bf16[64,256]{1,0:T(8,128)(2,1)} %clips_ref.1, bf16[8192,256]{1,0:T(8,128)(2,1)} %queue_hbm.1, s32[64]{0:T(128)} %pos_ref.1, f32[64]{0:T(128)} %cot_ref.1), custom_call_target="tpu_custom_call" | custom-call | flops 16999999488 | bytes 5000000 | tf_op jit(solution)/shard_map/pallas_call | solution.py:278
  54.8 1.5 %copy.6 = f32[64,256]{1,0:T(8,128)} copy(f32[64,256]{1,0:T(8,128)} %shard_map.46) | data formatting | bytes 131072

commit v3 on v2

--- a/solution.py
+++ b/solution.py
@@ -19,10 +19,13 @@
 KQ = 8192
 CH = 512
 PC = OWN + 8
-KB = 2048
-SK = 512
-STEPS = KQ // KB
 NCH = 4
+UNIT = 256
+UNITS = CH // UNIT * (KQ // UNIT)
+LAG_V = 2
+LAG_M = 3
+NS = 4
+NW = 3
 PARTS = 4
 
 
@@ -48,7 +51,7 @@
 
 
 def kernel(clips_ref, queue_hbm, pos_ref, cot_ref, out_ref,
-           q_ref, rec_ref, sc_ref, rows, acc, tacc, mbuf, pbuf, sbuf, abuf, prow, sq,
+           q_ref, rec_ref, sc_ref, rows, wbuf, tacc, mbuf, pbuf, sbuf, abuf, prow, sq,
            qsem, go_near, go_column, gs, gr, ps, pr, ms, mr, as_, ar, ss, sr):
     bank = lax.axis_index("bank")
     z = lax.axis_index("dp")
@@ -111,37 +114,43 @@
     eye = lax.broadcasted_iota(jnp.int32, (OWN, OWN), 0) == lax.broadcasted_iota(jnp.int32, (OWN, OWN), 1)
     local = (pos_ref[...] - bank * KQ).astype(F32).reshape(1, OWN)
     local_col = jnp.sum(jnp.where(eye, local, 0.0), axis=1, keepdims=True).astype(jnp.int32)
-    prow[...] = jnp.zeros_like(prow)
-    ones = jnp.ones((8, D), BF16)
-
-    def prep(k0, n):
-        qb = q_ref[pl.ds(k0, n), :]
+    ones = jnp.ones((16, D), BF16)
+
+    def prep_tile(k0, i, norms, picked):
+        k = pl.ds(pl.multiple_of(k0 + i * UNIT, UNIT), UNIT)
+        qb = q_ref[k, :]
         qf = qb.astype(F32)
         s2 = qf * qf
         hi = s2.astype(BF16)
         lo = (s2 - hi.astype(F32)).astype(BF16)
-        dims = (((1,), (1,)), ((), ()))
-        tot = lax.dot_general(ones, hi, dims, preferred_element_type=F32)
-        tot = tot + lax.dot_general(ones, lo, dims, preferred_element_type=F32)
-        r = lax.rsqrt(tot[0:1, :] + EPS)
-        rec_ref[:, pl.ds(k0, n)] = r
-        sc_ref[:, pl.ds(k0, n)] = r * (LOG2E * SHARP)
-        place = lax.broadcasted_iota(jnp.int32, (OWN, n), 1) + k0
+        place = lax.broadcasted_iota(jnp.int32, (OWN, UNIT), 1) + (k0 + i * UNIT)
         hot = jnp.where(place == local_col, 1.0, 0.0).astype(BF16)
-        prow[...] += jnp.dot(hot, qb, preferred_element_type=F32)
-
-    def prep_part(i):
-        queue_copy(i).wait()
+        for m, part in ((0, hi), (1, lo)):
+            pltpu.matmul_push_rhs(part, 0, m, transpose=True)
+            pltpu.matmul_acc_lhs(norms[m][i % 2], ones, load_staged_rhs=0)
+        pltpu.matmul_push_rhs(qb, 1, i % 2)
+        pltpu.matmul_acc_lhs(picked[i % 2], hot, load_staged_rhs=1)
+        total = pltpu.matmul_pop(norms[0][i % 2]) + pltpu.matmul_pop(norms[1][i % 2])
+        r = lax.rsqrt(total[0:1, :] + EPS)
+        rec_ref[:, k] = r
+        sc_ref[:, k] = r * (LOG2E * SHARP)
+
+    def prep(n0, n1, p0, p1):
         size = KQ // PARTS
 
-        def prep_step(k, _):
-            prep(pl.multiple_of(i * size + k * 512, 512), 512)
+        def part(p, _):
+            queue_copy(p).wait()
+            for i in range(size // UNIT):
+                prep_tile(p * size, i, (n0, n1), (p0, p1))
             return 0
 
-        lax.fori_loop(0, size // 512, prep_step, 0)
-
-    for i in range(PARTS):
-        prep_part(i)
+        lax.fori_loop(0, PARTS, part, 0)
+        prow[...] = pltpu.matmul_pop(p0) + pltpu.matmul_pop(p1)
+
+    def two_norms(m):
+        return [pltpu.ACC(m)((16, D), F32)] * 2
+
+    pl.run_scoped(prep, two_norms(0), two_norms(1), pltpu.ACC(0)((OWN, D), F32), pltpu.ACC(1)((OWN, D), F32))
 
     pl.semaphore_wait(go_near, len(NEAR))
     for t in (1, 2, 3):
@@ -167,12 +176,13 @@
         i = t * 4 + j
         return remote(sbuf.at[t, pl.ds(j * PC, PC)], abuf.at[i], as_.at[i], ar.at[i], chip(t, j))
 
-    def finish_chunk(t):
+    def finish_chunk(t, moments):
         for cc in range(2):
+            popped = pltpu.matmul_pop(moments[cc])
             for j in range(4):
+                dst = cc * half + j * PC
+                mbuf[t, dst:dst + OWN, :] = popped[j * OWN:(j + 1) * OWN, :]
                 src = (cc * 4 + j) * OWN
-                dst = cc * half + j * PC
-                mbuf[t, dst:dst + OWN, :] = acc[src:src + OWN, :]
                 col = jnp.sum(tacc[src:src + OWN, :], axis=1, keepdims=True)
                 row = jnp.sum(jnp.where(eye, col, 0.0), axis=0, keepdims=True)
                 mbuf[t, dst + OWN:dst + PC, :] = jnp.zeros((8, D), F32)
@@ -182,59 +192,78 @@
     def send_sums(t):
         to_partner(t).wait_recv()
         sbuf[t] = mbuf[t, pl.ds(mine0, half), :] + pbuf[t]
+        for t2 in range(NCH):
+            @pl.when(t == t2)
+            def _(t2=t2):
+                for j in range(4):
+                    if t2 or j:
+                        to_owner(t2, j).start()
+
+    def chunk(t, scores, moments):
+        tacc[...] = jnp.zeros_like(tacc)
+
+        def entries(u):
+            return pl.ds(u // 2 * UNIT, UNIT)
+
+        def start_scores(u):
+            part, stage = u % 2, u // 2 % 2
+            if part == 0:
+                pltpu.matmul_push_rhs(q_ref[entries(u), :], stage, 0, transpose=True)
+            pltpu.matmul_acc_lhs(scores[u % len(scores)], rows[t, part * UNIT:(part + 1) * UNIT, :],
+                                 load_staged_rhs=stage if part == 0 else None)
+
+        def exponential(u):
+            r = slice(u % 2 * UNIT, (u % 2 + 1) * UNIT)
+            e = jnp.exp2(pltpu.matmul_pop(scores[u % len(scores)]) * sc_ref[:, entries(u)])
+            tacc[r, :] = tacc[r, :] + (e[:, 0:128] + e[:, 128:256])
+            wbuf[u % NW] = (e * rec_ref[:, entries(u)]).astype(BF16)
+
+        def start_moments(u):
+            part, stage = u % 2, u // 2 % 2
+            if part == 0:
+                pltpu.matmul_push_rhs(q_ref[entries(u), :], stage, 1)
+            pltpu.matmul_acc_lhs(moments[part], wbuf[u % NW], load_staged_rhs=stage if part == 0 else None)
+
+        for s in range(UNITS + LAG_M):
+            if s < UNITS:
+                start_scores(s)
+            if 0 <= s - LAG_V < UNITS:
+                exponential(s - LAG_V)
+            if 0 <= s - LAG_M:
+                start_moments(s - LAG_M)
+            if s == 16:
+                @pl.when(t > 0)
+                def _():
+                    send_sums(t - 1)
+            if s == 56:
+                @pl.when(t == 0)
+                def _():
+                    pass_on(1)
+            if s == 28:
+                @pl.when(t == 1)
+                def _():
+                    pass_on(2)
+                    pass_on(3)
+
+        finish_chunk(t, moments)
+
+    def pass_on(t):
         for j in range(4):
-            if t or j:
-                to_owner(t, j).start()
-
-    def compute(t, s):
-        k0 = pl.multiple_of(s * KB, KB)
-        total = tacc[...]
-        rb = rows[t]
-        weights = []
-        for i in range(KB // SK):
-            k = pl.ds(k0 + i * SK, SK)
-            logits = lax.dot_general(rb, q_ref[k, :], (((1,), (1,)), ((), ())), preferred_element_type=F32)
-            e = jnp.exp2(logits * sc_ref[:, k])
-            for l in range(SK // 128):
-                total = total + e[:, l * 128:(l + 1) * 128]
-            weights.append((e * rec_ref[:, k]).astype(BF16))
-        tacc[...] = total
-        acc[...] += jnp.dot(jnp.concatenate(weights, axis=1), q_ref[pl.ds(k0, KB), :], preferred_element_type=F32)
-
-    def step(n, _):
-        t = n // STEPS
-        s = lax.rem(n, STEPS)
-
-        @pl.when(s == 0)
-        def _():
-            acc[...] = jnp.zeros_like(acc)
-            tacc[...] = jnp.zeros_like(tacc)
-
+            row_copy(t, j).wait_recv()
+        relay(t, 0, 4, t).start()
+
+    def chunks(*accumulators):
+        def body(t, _):
             @pl.when(t > 0)
             def _():
                 relay_wait(t, 0, 4, t)
 
-        compute(t, s)
-
-        for t2, after in ((1, 2), (2, 3), (3, 4)):
-            @pl.when(n == after)
-            def _(t2=t2):
-                for j in range(4):
-                    row_copy(t2, j).wait_recv()
-                relay(t2, 0, 4, t2).start()
-
-        for t2 in range(NCH - 1):
-            @pl.when(n == (t2 + 1) * STEPS)
-            def _(t2=t2):
-                send_sums(t2)
-
-        @pl.when(s == STEPS - 1)
-        def _():
-            finish_chunk(t)
-
-        return 0
-
-    lax.fori_loop(0, NCH * STEPS, step, 0)
+            chunk(t, accumulators[:NS], accumulators[NS:])
+            return 0
+
+        lax.fori_loop(0, NCH, body, 0)
+
+    pl.run_scoped(chunks, *[pltpu.ACC(0)((UNIT, D), F32)] * NS, *[pltpu.ACC(1)((UNIT, D), F32)] * 2)
     send_sums(NCH - 1)
     pl.semaphore_wait(go_column, len(COLUMN))
     prows = prow[...]
@@ -285,7 +314,7 @@
             pltpu.VMEM((1, KQ), F32),
             pltpu.VMEM((1, KQ), F32),
             pltpu.VMEM((NCH, CH, D), BF16),
-            pltpu.VMEM((CH, D), F32),
+            pltpu.VMEM((NW, UNIT, UNIT), BF16),
             pltpu.VMEM((CH, 128), F32),
             pltpu.VMEM((NCH, 8 * PC, D), F32),
             pltpu.VMEM((NCH, 4 * PC, D), F32),

time: 56.5 us -> 52.1 us (0.922)
  Pallas kernels: 54.8 us -> 50.4 us
    pallas_call x1, Pallas kernels: 54.8 us -> 50.4 us  [shards(): pl.pallas_call(kernel, out_shape=jax.ShapeDtypeStruct((OWN, D), F32), in_...]
where the time goes in v3:
time: 52.1 us; the launch traced here: 51.9 us
  Pallas kernels  50.4 us (97%)
  local copies, waits for them, and re-layouts  1.47 us (3%)
    pallas_call x1, Pallas kernels, shards(): pl.pallas_call(kernel, out_shape=jax.ShapeDtypeStruct((OWN, D), F32), in_...  50.4 us
    unnamed x1, local copies, waits for them, and re-layouts  1.47 us

profile of v3, /device:TPU:1, one launch (start us, length us, event | category | flops | bytes accessed | tf_op | source)
XLA Modules:
  0.0 51.9 jit_solution(521463815355650175)
XLA Ops:
  0.0 50.4 %shard_map.46 = f32[64,256]{1,0:T(8,128)} custom-call(bf16[64,256]{1,0:T(8,128)(2,1)} %clips_ref.1, bf16[8192,256]{1,0:T(8,128)(2,1)} %queue_hbm.1, s32[64]{0:T(128)} %pos_ref.1, f32[64]{0:T(128)} %cot_ref.1), custom_call_target="tpu_custom_call" | custom-call | flops 16999999488 | bytes 5000000 | tf_op jit(solution)/shard_map/pallas_call | solution.py:307
  50.4 1.5 %copy.6 = f32[64,256]{1,0:T(8,128)} copy(f32[64,256]{1,0:T(8,128)} %shard_map.46) | data formatting | bytes 131072

commit v4 on v3

--- a/solution.py
+++ b/solution.py
@@ -38,20 +38,21 @@
 
 
 CHUNKS = (
-    ((0, 0), (1, 1), (1, 3), (3, 1)),
-    ((3, 3), (2, 0), (0, 2), (2, 2)),
-    ((2, 1), (2, 3), (1, 2), (3, 2)),
+    ((0, 0), (2, 0), (0, 2), (3, 3)),
+    ((2, 2), (2, 3), (1, 2), (3, 2)),
+    ((1, 1), (1, 3), (3, 1), (2, 1)),
     ((1, 0), (3, 0), (0, 1), (0, 3)),
 )
-NEAR = [(dx, dy, 0, 0) for dx in (0, 1, 3) for dy in (0, 1, 3) if dx or dy]
+NEAR = [(dx, dy, 0, 0) for dx in (0, 1, 3) for dy in (0, 1, 3) if dx or dy] + [(2, 0, 0, 0), (0, 2, 0, 0)]
+KNOWN = 0
 COLUMN = [(0, 0, dc, dz) for dc in range(2) for dz in range(4) if dc or dz]
 ALL = sorted(
     [(dx, dy, dc, dz) for dx in range(4) for dy in range(4) for dc in range(2) for dz in range(4) if dx or dy or dc or dz],
     key=lambda o: -hops(o))
 
 
-def kernel(clips_ref, queue_hbm, pos_ref, cot_ref, out_ref,
-           q_ref, rec_ref, sc_ref, rows, wbuf, tacc, mbuf, pbuf, sbuf, abuf, prow, sq,
+def kernel(clips_hbm, queue_hbm, pos_hbm, cot_hbm, out_ref,
+           clips_ref, pos_ref, cot_ref, isem, q_ref, rec_ref, sc_ref, rows, wbuf, tacc, mbuf, pbuf, sbuf, abuf, prow, sq,
            qsem, go_near, go_column, gs, gr, ps, pr, ms, mr, as_, ar, ss, sr):
     bank = lax.axis_index("bank")
     z = lax.axis_index("dp")
@@ -59,12 +60,14 @@
     y = lax.rem(bank // 2, 4)
     x = bank // 8
 
+    at_x = [lax.rem(x + d, 4) * 8 for d in range(4)]
+    at_y = [lax.rem(y + d, 4) * 2 for d in range(4)]
+    at_c = [c, 1 - c]
+    at_z = [lax.rem(z + d, 4) for d in range(4)]
+
     def device(o):
         dx, dy, dc, dz = o
-        bx = lax.rem(x + dx, 4) if dx else x
-        by = lax.rem(y + dy, 4) if dy else y
-        bc = 1 - c if dc else c
-        return ((bx * 4 + by) * 2 + bc, lax.rem(z + dz, 4) if dz else z)
+        return (at_x[dx] + at_y[dy] + at_c[dc], at_z[dz])
 
     def chip(t, j, back=False):
         dx, dy = CHUNKS[t][j]
@@ -81,9 +84,14 @@
     barrier = pltpu.get_barrier_semaphore()
     for o in NEAR + COLUMN:
         pl.semaphore_signal(barrier, inc=1, device_id=device(o), device_id_type=MESH)
+    inputs = [pltpu.make_async_copy(src, dst, isem.at[i])
+              for i, (src, dst) in enumerate(((clips_hbm, clips_ref), (pos_hbm, pos_ref), (cot_hbm, cot_ref)))]
+    for copy in inputs:
+        copy.start()
     for i in range(PARTS):
         queue_copy(i).start()
 
+    inputs[0].wait()
     raw = clips_ref[...].astype(F32)
     inv = inverse_norms(raw)
     dirs = raw * inv
@@ -108,9 +116,13 @@
     for j in (1, 2, 3):
         row_copy(0, j).start()
     relay(0, 0, 1, 4).start()
+    for j in range(KNOWN):
+        row_copy(1, j).start()
     for o in NEAR:
         pl.semaphore_signal(go_near, inc=1, device_id=device(o), device_id_type=MESH)
 
+    inputs[1].wait()
+    inputs[2].wait()
     eye = lax.broadcasted_iota(jnp.int32, (OWN, OWN), 0) == lax.broadcasted_iota(jnp.int32, (OWN, OWN), 1)
     local = (pos_ref[...] - bank * KQ).astype(F32).reshape(1, OWN)
     local_col = jnp.sum(jnp.where(eye, local, 0.0), axis=1, keepdims=True).astype(jnp.int32)
@@ -153,9 +165,8 @@
     pl.run_scoped(prep, two_norms(0), two_norms(1), pltpu.ACC(0)((OWN, D), F32), pltpu.ACC(1)((OWN, D), F32))
 
     pl.semaphore_wait(go_near, len(NEAR))
-    for t in (1, 2, 3):
-        for j in range(4):
-            row_copy(t, j).start()
+    for j in range(KNOWN, 4):
+        row_copy(1, j).start()
     for o in COLUMN:
         pl.semaphore_signal(go_column, inc=1, device_id=device(o), device_id_type=MESH)
 
@@ -231,18 +242,27 @@
                 exponential(s - LAG_V)
             if 0 <= s - LAG_M:
                 start_moments(s - LAG_M)
-            if s == 16:
+            if s == 20:
                 @pl.when(t > 0)
                 def _():
                     send_sums(t - 1)
-            if s == 56:
+            if s == 24:
                 @pl.when(t == 0)
                 def _():
+                    for t2 in (2, 3):
+                        for j in range(4):
+                            row_copy(t2, j).start()
+            if s == 62:
+                @pl.when(t == 0)
+                def _():
                     pass_on(1)
-            if s == 28:
+            if s == 36:
                 @pl.when(t == 1)
                 def _():
                     pass_on(2)
+
+                @pl.when(t == 2)
+                def _():
                     pass_on(3)
 
         finish_chunk(t, moments)
@@ -306,10 +326,14 @@
     dma = pltpu.SemaphoreType.DMA
     return pl.pallas_call(
         kernel,
-        out_shape=jax.ShapeDtypeStruct((OWN, D), F32),
-        in_specs=[vmem, pl.BlockSpec(memory_space=pl.ANY), vmem, vmem],
+        out_shape=pltpu.VMEM((OWN, D), F32),
+        in_specs=[pl.BlockSpec(memory_space=pl.ANY)] * 4,
         out_specs=vmem,
         scratch_shapes=[
+            pltpu.VMEM((OWN, D), BF16),
+            pltpu.VMEM((OWN,), jnp.int32),
+            pltpu.VMEM((OWN,), F32),
+            dma((3,)),
             pltpu.VMEM((KQ, D), BF16),
             pltpu.VMEM((1, KQ), F32),
             pltpu.VMEM((1, KQ), F32),

time: 52.1 us -> 48.3 us (0.927)
  Pallas kernels: 50.4 us -> 47.5 us
  local copies, waits for them, and re-layouts: 1.47 us -> 0.63 us
    pallas_call x1, Pallas kernels: 50.4 us -> 47.5 us  [shards(): pl.pallas_call(kernel, out_shape=pltpu.VMEM((OWN, D), F32), in_specs=[pl....]
    unnamed x1, local copies, waits for them, and re-layouts: 1.47 us -> 0.63 us
where the time goes in v4:
time: 48.3 us; the launch traced here: 48.2 us
  Pallas kernels  47.5 us (98%)
  local copies, waits for them, and re-layouts  0.63 us (1%)
    pallas_call x1, Pallas kernels, shards(): pl.pallas_call(kernel, out_shape=pltpu.VMEM((OWN, D), F32), in_specs=[pl....  47.5 us

profile of v4, /device:TPU:1, one launch (start us, length us, event | category | flops | bytes accessed | tf_op | source)
XLA Modules:
  0.0 48.2 jit_solution(15687201204580514353)
XLA Ops:
  0.0 47.5 %shard_map.46 = f32[64,256]{1,0:T(8,128)S(1)} custom-call(bf16[64,256]{1,0:T(8,128)(2,1)} %clips_hbm.1, bf16[8192,256]{1,0:T(8,128)(2,1)} %queue_hbm.1, s32[64]{0:T(128)} %pos_hbm.1, f32[64]{0:T(128)} %cot_hbm.1), custom_call_target="tpu_custom_call" | custom-call | flops 16999999488 | bytes 5000000 | tf_op jit(solution)/shard_map/pallas_call | solution.py:327
  47.5 0.6 %copy.6 = f32[64,256]{1,0:T(8,128)} copy(f32[64,256]{1,0:T(8,128)S(1)} %shard_map.46) | data formatting | bytes 131072

commit v5 on v4

v5 whole, which is shorter than its diff:
```python
import math

import jax
import jax.numpy as jnp
from jax import lax
from jax.experimental import pallas as pl
from jax.experimental.pallas import tpu as pltpu
from jax.sharding import PartitionSpec as P

MESH = pl.DeviceIdType.MESH
LOG2E = 1.4426950408889634
SHARP = 1.0 / 0.07
EPS = 1e-6
F32 = jnp.float32
BF16 = jnp.bfloat16

OWN = 64
D = 256
KQ = 8192
CH = 256
PC = OWN + 8
NCH = 4
UNIT = 256
UNITS = 2 * KQ // UNIT
LAG_V = 2
LAG_M = 3
NS = 4
NW = 3
PARTS = 4


def inverse_norms(v):
    return lax.rsqrt(jnp.sum(v * v, axis=1, keepdims=True) + EPS)


def hops(o):
    return sum(min(v, 4 - v) for v in (o[0] % 4, o[1] % 4, o[3] % 4))


CHUNKS = (
    ((0, 0), (2, 0), (0, 2), (3, 3)),
    ((2, 2), (2, 3), (1, 2), (3, 2)),
    ((1, 1), (1, 3), (3, 1), (2, 1)),
    ((1, 0), (3, 0), (0, 1), (0, 3)),
)
NEAR = [(dx, dy, 0, 0) for dx in (0, 1, 3) for dy in (0, 1, 3) if dx or dy] + [(2, 0, 0, 0), (0, 2, 0, 0)]
SEND_LATER = 24
KNOWN = 0
COLUMN = [(0, 0, dc, dz) for dc in range(2) for dz in range(4) if dc or dz]
ALL = sorted(
    [(dx, dy, dc, dz) for dx in range(4) for dy in range(4) for dc in range(2) for dz in range(4) if dx or dy or dc or dz],
    key=lambda o: -hops(o))


def kernel(clips_hbm, queue_hbm, pos_hbm, cot_hbm, out_ref,
           clips_ref, pos_ref, cot_ref, q_ref, rec_ref, rows, wbuf, tacc, sbuf, abuf, prow, sq,
           isem, qsem, go_near, go_column, qs, qr, ns, nr, gs, gr, as_, ar, ss, sr):
    bank = lax.axis_index("bank")
    z = lax.axis_index("dp")
    c = lax.rem(bank, 2)
    y = lax.rem(bank // 2, 4)
    x = bank // 8

    at_x = [lax.rem(x + d, 4) * 8 for d in range(4)]
    at_y = [lax.rem(y + d, 4) * 2 for d in range(4)]
    at_c = [c, 1 - c]
    at_z = [lax.rem(z + d, 4) for d in range(4)]

    def device(o):
        dx, dy, dc, dz = o
        return (at_x[dx] + at_y[dy] + at_c[dc], at_z[dz])

    def chip(t, j, back=False):
        dx, dy = CHUNKS[t][j]
        return device(((4 - dx) % 4, (4 - dy) % 4, 0, 0) if back else (dx, dy, 0, 0))

    def remote(src, dst, s, r, dev):
        return pltpu.make_async_remote_copy(
            src_ref=src, dst_ref=dst, send_sem=s, recv_sem=r, device_id=dev, device_id_type=MESH)

    def queue_copy(i):
        part = pl.ds(i * (KQ // PARTS), KQ // PARTS)
        return pltpu.make_async_copy(queue_hbm.at[part], q_ref.at[part], qsem.at[i])

    barrier = pltpu.get_barrier_semaphore()
    for o in NEAR + COLUMN:
        pl.semaphore_signal(barrier, inc=1, device_id=device(o), device_id_type=MESH)
    inputs = [pltpu.make_async_copy(src, dst, isem.at[i])
              for i, (src, dst) in enumerate(((clips_hbm, clips_ref), (pos_hbm, pos_ref), (cot_hbm, cot_ref)))]
    for copy in inputs:
        copy.start()
    for i in range(PARTS):
        queue_copy(i).start()

    inputs[0].wait()
    raw = clips_ref[...].astype(F32)
    inv = inverse_norms(raw)
    dirs = raw * inv
    rows[0, 0:OWN, :] = dirs.astype(BF16)

    pl.semaphore_wait(barrier, len(NEAR) + len(COLUMN))

    def row_copy(t, j):
        return remote(rows.at[0, pl.ds(0, OWN)], rows.at[t, pl.ds(j * OWN, OWN)],
                      gs.at[t * 4 + j], gr.at[t * 4 + j], chip(t, j, back=True))

    partner = device((0, 0, 1, 0))

    def queue_to_partner(i):
        size = KQ // PARTS
        return remote(queue_hbm.at[pl.ds(i * size, size)], q_ref.at[pl.ds(KQ + i * size, size)], qs.at[i], qr.at[i], partner)

    def norms_to_partner():
        return remote(rec_ref.at[:, pl.ds(0, KQ)], rec_ref.at[:, pl.ds(KQ, KQ)], ns, nr, partner)

    for j in (1, 2, 3):
        row_copy(0, j).start()
    for j in range(KNOWN):
        row_copy(1, j).start()
    for i in range(PARTS):
        queue_to_partner(i).start()
    for o in NEAR:
        pl.semaphore_signal(go_near, inc=1, device_id=device(o), device_id_type=MESH)

    inputs[1].wait()
    inputs[2].wait()
    eye = lax.broadcasted_iota(jnp.int32, (OWN, OWN), 0) == lax.broadcasted_iota(jnp.int32, (OWN, OWN), 1)
    local = (pos_ref[...] - bank * KQ).astype(F32).reshape(1, OWN)
    local_col = jnp.sum(jnp.where(eye, local, 0.0), axis=1, keepdims=True).astype(jnp.int32)
    ones = jnp.ones((16, D), BF16)

    def prep_tile(k0, i, norms, picked):
        k = pl.ds(pl.multiple_of(k0 + i * UNIT, UNIT), UNIT)
        qb = q_ref[k, :]
        qf = qb.astype(F32)
        s2 = qf * qf
        hi = s2.astype(BF16)
        lo = (s2 - hi.astype(F32)).astype(BF16)
        place = lax.broadcasted_iota(jnp.int32, (OWN, UNIT), 1) + (k0 + i * UNIT)
        hot = jnp.where(place == local_col, 1.0, 0.0).astype(BF16)
        for m, part in ((0, hi), (1, lo)):
            pltpu.matmul_push_rhs(part, 0, m, transpose=True)
            pltpu.matmul_acc_lhs(norms[m][i % 2], ones, load_staged_rhs=0)
        pltpu.matmul_push_rhs(qb, 1, i % 2)
        pltpu.matmul_acc_lhs(picked[i % 2], hot, load_staged_rhs=1)
        total = pltpu.matmul_pop(norms[0][i % 2]) + pltpu.matmul_pop(norms[1][i % 2])
        rec_ref[:, k] = lax.rsqrt(total[0:1, :] + EPS)

    def prep(n0, n1, p0, p1):
        size = KQ // PARTS

        def part(p, _):
            queue_copy(p).wait()
            for i in range(size // UNIT):
                prep_tile(p * size, i, (n0, n1), (p0, p1))
            return 0

        lax.fori_loop(0, PARTS, part, 0)
        prow[...] = pltpu.matmul_pop(p0) + pltpu.matmul_pop(p1)

    def two_norms(m):
        return [pltpu.ACC(m)((16, D), F32)] * 2

    pl.run_scoped(prep, two_norms(0), two_norms(1), pltpu.ACC(0)((OWN, D), F32), pltpu.ACC(1)((OWN, D), F32))

    norms_to_partner().start()

    pl.semaphore_wait(go_near, len(NEAR))
    for j in range(KNOWN, 4):
        row_copy(1, j).start()
    for o in COLUMN:
        pl.semaphore_signal(go_column, inc=1, device_id=device(o), device_id_type=MESH)

    def to_owner(t, j):
        i = t * 4 + j
        return remote(sbuf.at[t, pl.ds(j * PC, PC)], abuf.at[i], as_.at[i], ar.at[i], chip(t, j))

    def finish_chunk(t, moments):
        popped = pltpu.matmul_pop(moments)
        for j in range(4):
            src, dst = j * OWN, j * PC
            sbuf[t, dst:dst + OWN, :] = popped[src:src + OWN, :]
            col = jnp.sum(tacc[src:src + OWN, :], axis=1, keepdims=True)
            row = jnp.sum(jnp.where(eye, col, 0.0), axis=0, keepdims=True)
            sbuf[t, dst + OWN:dst + PC, :] = jnp.zeros((8, D), F32)
            sbuf[t, dst + OWN:dst + PC, 0:OWN] = jnp.broadcast_to(row, (8, OWN))
        for t2 in range(NCH):
            @pl.when(t == t2)
            def _(t2=t2):
                for j in range(4):
                    if t2 or j:
                        to_owner(t2, j).start()

    def chunk(t, scores, moments):
        tacc[...] = jnp.zeros_like(tacc)

        def entries(u):
            return pl.ds(u * UNIT, UNIT)

        def start_scores(u):
            pltpu.matmul_push_rhs(q_ref[entries(u), :], u % 2, 0, transpose=True)
            pltpu.matmul_acc_lhs(scores[u % NS], rows[t], load_staged_rhs=u % 2)

        def exponential(u):
            r = rec_ref[:, entries(u)]
            e = jnp.exp2(pltpu.matmul_pop(scores[u % NS]) * (r * (LOG2E * SHARP)))
            tacc[...] = tacc[...] + (e[:, 0:128] + e[:, 128:256])
            wbuf[u % NW] = (e * r).astype(BF16)

        def start_moments(u):
            pltpu.matmul_push_rhs(q_ref[entries(u), :], u % 2, 1)
            pltpu.matmul_acc_lhs(moments, wbuf[u % NW], load_staged_rhs=u % 2)

        for s in range(UNITS + LAG_M):
            if s == SEND_LATER:
                @pl.when(t == 0)
                def _():
                    for t2 in (2, 3):
                        for j in range(4):
                            row_copy(t2, j).start()
            if s == UNITS // 2:
                @pl.when(t == 0)
                def _():
                    norms_to_partner().wait_recv()
                    for i in range(PARTS // 2):
                        queue_to_partner(i).wait_recv()
            if s == UNITS * 3 // 4:
                @pl.when(t == 0)
                def _():
                    for i in range(PARTS // 2, PARTS):
                        queue_to_partner(i).wait_recv()
            if s < UNITS:
                start_scores(s)
            if 0 <= s - LAG_V < UNITS:
                exponential(s - LAG_V)
            if 0 <= s - LAG_M:
                start_moments(s - LAG_M)

        finish_chunk(t, moments)

    def chunks(*accumulators):
        def body(t, _):
            for t2 in range(NCH):
                @pl.when(t == t2)
                def _(t2=t2):
                    for j in range(4):
                        if t2 or j:
                            row_copy(t2, j).wait_recv()

            chunk(t, accumulators[:NS], accumulators[NS])
            return 0

        lax.fori_loop(0, NCH, body, 0)

    pl.run_scoped(chunks, *[pltpu.ACC(0)((UNIT, D), F32)] * NS, pltpu.ACC(1)((UNIT, D), F32))
    pl.semaphore_wait(go_column, len(COLUMN))
    prows = prow[...]
    pushed_away = inverse_norms(prows) * prows
    cot = jnp.sum(jnp.where(eye, cot_ref[...].reshape(1, OWN), 0.0), axis=1, keepdims=True)
    own = sbuf[0, 0:PC, :]
    for i in range(1, 16):
        to_owner(i // 4, i % 4).wait_recv()
        own = own + abuf[i]
    totals = jnp.sum(jnp.where(eye, own[OWN:OWN + 1, 0:OWN], 0.0), axis=1, keepdims=True)
    pushed = own[0:OWN, :] / totals - pushed_away
    tangent = pushed - dirs * jnp.sum(dirs * pushed, axis=1, keepdims=True)
    gradient = cot * tangent * inv

    squares = jnp.sum(gradient * gradient, axis=0, keepdims=True)
    sq[0] = squares[:, 0:128] + squares[:, 128:256]
    for i, o in enumerate(ALL):
        remote(sq.at[0], sq.at[i + 1], ss, sr, device(o)).start()
    others = sq.at[pl.ds(1, len(ALL))]
    remote(others, others, ss, sr, device((0, 0, 1, 0))).wait()
    squares = jnp.sum(jnp.sum(sq[...], axis=0), axis=1, keepdims=True)
    clip_total = OWN * lax.axis_size("bank") * lax.axis_size("dp")
    factor = jnp.minimum(1.0, (4.0 * math.sqrt(clip_total)) / jnp.sqrt(squares + EPS))
    out_ref[...] = gradient * factor

    for i in range(1, 16):
        row_copy(i // 4, i % 4).wait_send()
        to_owner(i // 4, i % 4).wait_send()
    for i in range(PARTS):
        queue_to_partner(i).wait_send()
    norms_to_partner().wait_send()


def shards(clips, queue, positive, cotangent):
    vmem = pl.BlockSpec(memory_space=pltpu.VMEM)
    dma = pltpu.SemaphoreType.DMA
    return pl.pallas_call(
        kernel,
        out_shape=pltpu.VMEM((OWN, D), F32),
        in_specs=[pl.BlockSpec(memory_space=pl.ANY)] * 4,
        out_specs=vmem,
        scratch_shapes=[
            pltpu.VMEM((OWN, D), BF16),
            pltpu.VMEM((OWN,), jnp.int32),
            pltpu.VMEM((OWN,), F32),
            pltpu.VMEM((2 * KQ, D), BF16),
            pltpu.VMEM((1, 2 * KQ), F32),
            pltpu.VMEM((NCH, CH, D), BF16),
            pltpu.VMEM((NW, UNIT, UNIT), BF16),
            pltpu.VMEM((CH, 128), F32),
            pltpu.VMEM((NCH, 4 * PC, D), F32),
            pltpu.VMEM((16, PC, D), F32),
            pltpu.VMEM((OWN, D), F32),
            pltpu.VMEM((len(ALL) + 1, 1, 128), F32),
            dma((3,)),
            dma((PARTS,)),
            pltpu.SemaphoreType.REGULAR, pltpu.SemaphoreType.REGULAR,
            dma((PARTS,)), dma((PARTS,)),
            dma, dma,
            dma((16,)), dma((16,)),
            dma((16,)), dma((16,)),
            dma, dma,
        ],
        compiler_params=pltpu.CompilerParams(
            collective_id=0, has_side_effects=True, vmem_limit_bytes=56 << 20),
        cost_estimate=pl.CostEstimate(flops=17 * 10**9, bytes_accessed=5 * 10**6, transcendentals=17 * 10**6),
    )(clips, queue, positive, cotangent)


def solution(mesh):
    in_specs = (P(("bank", "dp"), None), P("bank", None), P(("bank", "dp")), P(("bank", "dp")))
    return jax.shard_map(shards, mesh=mesh, in_specs=in_specs, out_specs=P(("bank", "dp"), None), check_vma=False)
```

time: 48.3 us -> 44.9 us (0.930)
  Pallas kernels: 47.5 us -> 44.2 us
    pallas_call x1, Pallas kernels: 47.5 us -> 44.2 us  [shards(): pl.pallas_call(kernel, out_shape=pltpu.VMEM((OWN, D), F32), in_specs=[pl....]
where the time goes in v5:
time: 44.9 us; the launch traced here: 44.8 us
  Pallas kernels  44.2 us (98%)
  local copies, waits for them, and re-layouts  0.63 us (1%)
    pallas_call x1, Pallas kernels, shards(): pl.pallas_call(kernel, out_shape=pltpu.VMEM((OWN, D), F32), in_specs=[pl....  44.2 us

profile of v5, /device:TPU:1, one launch (start us, length us, event | category | flops | bytes accessed | tf_op | source)
XLA Modules:
  0.0 44.8 jit_solution(17990024640043745946)
XLA Ops:
  0.0 44.2 %shard_map.46 = f32[64,256]{1,0:T(8,128)S(1)} custom-call(bf16[64,256]{1,0:T(8,128)(2,1)} %clips_hbm.1, bf16[8192,256]{1,0:T(8,128)(2,1)} %queue_hbm.1, s32[64]{0:T(128)} %pos_hbm.1, f32[64]{0:T(128)} %cot_hbm.1), custom_call_target="tpu_custom_call" | custom-call | flops 16999999488 | bytes 5000000 | tf_op jit(solution)/shard_map/pallas_call | solution.py:291
  44.2 0.6 %copy.6 = f32[64,256]{1,0:T(8,128)} copy(f32[64,256]{1,0:T(8,128)S(1)} %shard_map.46) | data formatting | bytes 131072

commit v6 on v5

--- a/solution.py
+++ b/solution.py
@@ -25,7 +25,9 @@
 LAG_V = 2
 LAG_M = 3
 NS = 4
-NW = 3
+NW = 4
+QUEUE_WAITS = {32: (0, 1), 44: (2,), 54: (3,)}
+SEND = 6
 PARTS = 4
 
 
@@ -175,70 +177,41 @@
         i = t * 4 + j
         return remote(sbuf.at[t, pl.ds(j * PC, PC)], abuf.at[i], as_.at[i], ar.at[i], chip(t, j))
 
-    def finish_chunk(t, moments):
+    def finish_chunk(t, slot, moments):
         popped = pltpu.matmul_pop(moments)
         for j in range(4):
             src, dst = j * OWN, j * PC
             sbuf[t, dst:dst + OWN, :] = popped[src:src + OWN, :]
-            col = jnp.sum(tacc[src:src + OWN, :], axis=1, keepdims=True)
+            col = jnp.sum(tacc[slot, src:src + OWN, :], axis=1, keepdims=True)
             row = jnp.sum(jnp.where(eye, col, 0.0), axis=0, keepdims=True)
             sbuf[t, dst + OWN:dst + PC, :] = jnp.zeros((8, D), F32)
             sbuf[t, dst + OWN:dst + PC, 0:OWN] = jnp.broadcast_to(row, (8, OWN))
-        for t2 in range(NCH):
-            @pl.when(t == t2)
-            def _(t2=t2):
-                for j in range(4):
-                    if t2 or j:
-                        to_owner(t2, j).start()
-
-    def chunk(t, scores, moments):
+
+    def chunks(*accumulators):
+        scores, moments = accumulators[:NS], accumulators[NS]
+        wbuf[...] = jnp.zeros_like(wbuf)
         tacc[...] = jnp.zeros_like(tacc)
 
-        def entries(u):
-            return pl.ds(u * UNIT, UNIT)
-
-        def start_scores(u):
-            pltpu.matmul_push_rhs(q_ref[entries(u), :], u % 2, 0, transpose=True)
+        def entries(t, u):
+            if u >= 0:
+                return pl.ds(u * UNIT, UNIT)
+            return pl.ds(pl.multiple_of(lax.min(t, 1) * (UNITS + u) * UNIT, UNIT), UNIT)
+
+        def start_scores(t, u):
+            pltpu.matmul_push_rhs(q_ref[entries(t, u), :], u % 2, 0, transpose=True)
             pltpu.matmul_acc_lhs(scores[u % NS], rows[t], load_staged_rhs=u % 2)
 
-        def exponential(u):
-            r = rec_ref[:, entries(u)]
+        def exponential(t, u):
+            slot = lax.rem(t, 2) if u >= 0 else lax.rem(t + 1, 2)
+            r = rec_ref[:, entries(t, u)]
             e = jnp.exp2(pltpu.matmul_pop(scores[u % NS]) * (r * (LOG2E * SHARP)))
-            tacc[...] = tacc[...] + (e[:, 0:128] + e[:, 128:256])
+            tacc[slot] = tacc[slot] + (e[:, 0:128] + e[:, 128:256])
             wbuf[u % NW] = (e * r).astype(BF16)
 
-        def start_moments(u):
-            pltpu.matmul_push_rhs(q_ref[entries(u), :], u % 2, 1)
+        def start_moments(t, u):
+            pltpu.matmul_push_rhs(q_ref[entries(t, u), :], u % 2, 1)
             pltpu.matmul_acc_lhs(moments, wbuf[u % NW], load_staged_rhs=u % 2)
 
-        for s in range(UNITS + LAG_M):
-            if s == SEND_LATER:
-                @pl.when(t == 0)
-                def _():
-                    for t2 in (2, 3):
-                        for j in range(4):
-                            row_copy(t2, j).start()
-            if s == UNITS // 2:
-                @pl.when(t == 0)
-                def _():
-                    norms_to_partner().wait_recv()
-                    for i in range(PARTS // 2):
-                        queue_to_partner(i).wait_recv()
-            if s == UNITS * 3 // 4:
-                @pl.when(t == 0)
-                def _():
-                    for i in range(PARTS // 2, PARTS):
-                        queue_to_partner(i).wait_recv()
-            if s < UNITS:
-                start_scores(s)
-            if 0 <= s - LAG_V < UNITS:
-                exponential(s - LAG_V)
-            if 0 <= s - LAG_M:
-                start_moments(s - LAG_M)
-
-        finish_chunk(t, moments)
-
-    def chunks(*accumulators):
         def body(t, _):
             for t2 in range(NCH):
                 @pl.when(t == t2)
@@ -247,10 +220,45 @@
                         if t2 or j:
                             row_copy(t2, j).wait_recv()
 
-            chunk(t, accumulators[:NS], accumulators[NS])
+            for s in range(UNITS):
+                if s == SEND:
+                    for t2 in range(NCH - 1):
+                        @pl.when(t == t2 + 1)
+                        def _(t2=t2):
+                            for j in range(4):
+                                if t2 or j:
+                                    to_owner(t2, j).start()
+                if s == SEND_LATER:
+                    @pl.when(t == 0)
+                    def _():
+                        for t2 in (2, 3):
+                            for j in range(4):
+                                row_copy(t2, j).start()
+                if s in QUEUE_WAITS:
+                    @pl.when(t == 0)
+                    def _(s=s):
+                        if s == UNITS // 2:
+                            norms_to_partner().wait_recv()
+                        for i in QUEUE_WAITS[s]:
+                            queue_to_partner(i).wait_recv()
+                start_scores(t, s)
+                if s == LAG_V:
+                    tacc[lax.rem(t, 2)] = jnp.zeros((CH, 128), F32)
+                exponential(t, s - LAG_V)
+                start_moments(t, s - LAG_M)
+                if s == LAG_M - 1:
+                    finish_chunk(lax.max(t - 1, 0), lax.rem(t + 1, 2), moments)
             return 0
 
         lax.fori_loop(0, NCH, body, 0)
+        last = NCH - 1
+        for s in range(UNITS, UNITS + LAG_M):
+            if s - LAG_V < UNITS:
+                exponential(last, s - LAG_V)
+            start_moments(last, s - LAG_M)
+        finish_chunk(last, last % 2, moments)
+        for j in range(4):
+            to_owner(last, j).start()
 
     pl.run_scoped(chunks, *[pltpu.ACC(0)((UNIT, D), F32)] * NS, pltpu.ACC(1)((UNIT, D), F32))
     pl.semaphore_wait(go_column, len(COLUMN))
@@ -301,7 +309,7 @@
             pltpu.VMEM((1, 2 * KQ), F32),
             pltpu.VMEM((NCH, CH, D), BF16),
             pltpu.VMEM((NW, UNIT, UNIT), BF16),
-            pltpu.VMEM((CH, 128), F32),
+            pltpu.VMEM((2, CH, 128), F32),
             pltpu.VMEM((NCH, 4 * PC, D), F32),
             pltpu.VMEM((16, PC, D), F32),
             pltpu.VMEM((OWN, D), F32),

time: 44.9 us -> 44.5 us (level)
  no operation moved by 1% of the time
where the time goes in v6:
time: 44.5 us; the launch traced here: 44.4 us
  Pallas kernels  43.8 us (98%)
  local copies, waits for them, and re-layouts  0.63 us (1%)
    pallas_call x1, Pallas kernels, shards(): pl.pallas_call(kernel, out_shape=pltpu.VMEM((OWN, D), F32), in_specs=[pl....  43.8 us

profile of v6, /device:TPU:1, one launch (start us, length us, event | category | flops | bytes accessed | tf_op | source)
XLA Modules:
  0.0 44.4 jit_solution(4105947941625160857)
XLA Ops:
  0.0 43.8 %shard_map.46 = f32[64,256]{1,0:T(8,128)S(1)} custom-call(bf16[64,256]{1,0:T(8,128)(2,1)} %clips_hbm.1, bf16[8192,256]{1,0:T(8,128)(2,1)} %queue_hbm.1, s32[64]{0:T(128)} %pos_hbm.1, f32[64]{0:T(128)} %cot_hbm.1), custom_call_target="tpu_custom_call" | custom-call | flops 16999999488 | bytes 5000000 | tf_op jit(solution)/shard_map/pallas_call | solution.py:299
  43.8 0.6 %copy.6 = f32[64,256]{1,0:T(8,128)} copy(f32[64,256]{1,0:T(8,128)S(1)} %shard_map.46) | data formatting | bytes 131072

commit v7 on v6

--- a/solution.py
+++ b/solution.py
@@ -18,7 +18,6 @@
 D = 256
 KQ = 8192
 CH = 256
-PC = OWN + 8
 NCH = 4
 UNIT = 256
 UNITS = 2 * KQ // UNIT
@@ -55,8 +54,8 @@
 
 
 def kernel(clips_hbm, queue_hbm, pos_hbm, cot_hbm, out_ref,
-           clips_ref, pos_ref, cot_ref, q_ref, rec_ref, rows, wbuf, tacc, sbuf, abuf, prow, sq,
-           isem, qsem, go_near, go_column, qs, qr, ns, nr, gs, gr, as_, ar, ss, sr):
+           clips_ref, pos_ref, cot_ref, q_ref, rec_ref, rows, wbuf, tacc, sbuf, abuf, tsend, tgot, prow, sq,
+           isem, qsem, go_near, go_column, qs, qr, ns, nr, gs, gr, as_, ar, ts, tr, ss, sr):
     bank = lax.axis_index("bank")
     z = lax.axis_index("dp")
     c = lax.rem(bank, 2)
@@ -127,6 +126,7 @@
     inputs[1].wait()
     inputs[2].wait()
     eye = lax.broadcasted_iota(jnp.int32, (OWN, OWN), 0) == lax.broadcasted_iota(jnp.int32, (OWN, OWN), 1)
+    wide_eye = lax.broadcasted_iota(jnp.int32, (OWN, 128), 0) == lax.broadcasted_iota(jnp.int32, (OWN, 128), 1)
     local = (pos_ref[...] - bank * KQ).astype(F32).reshape(1, OWN)
     local_col = jnp.sum(jnp.where(eye, local, 0.0), axis=1, keepdims=True).astype(jnp.int32)
     ones = jnp.ones((16, D), BF16)
@@ -173,19 +173,31 @@
     for o in COLUMN:
         pl.semaphore_signal(go_column, inc=1, device_id=device(o), device_id_type=MESH)
 
-    def to_owner(t, j):
-        i = t * 4 + j
-        return remote(sbuf.at[t, pl.ds(j * PC, PC)], abuf.at[i], as_.at[i], ar.at[i], chip(t, j))
+    class to_owner:
+        def __init__(self, t, j):
+            i = t * 4 + j
+            dev = chip(t, j)
+            self.copies = (
+                remote(tsend.at[i], tgot.at[i], ts.at[i], tr.at[i], dev),
+                remote(sbuf.at[t, pl.ds(j * OWN, OWN)], abuf.at[i], as_.at[i], ar.at[i], dev))
+
+        def start(self):
+            for copy in self.copies:
+                copy.start()
+
+        def wait_recv(self):
+            for copy in self.copies:
+                copy.wait_recv()
+
+        def wait_send(self):
+            for copy in self.copies:
+                copy.wait_send()
 
     def finish_chunk(t, slot, moments):
-        popped = pltpu.matmul_pop(moments)
+        sbuf[t] = pltpu.matmul_pop(moments)
         for j in range(4):
-            src, dst = j * OWN, j * PC
-            sbuf[t, dst:dst + OWN, :] = popped[src:src + OWN, :]
-            col = jnp.sum(tacc[slot, src:src + OWN, :], axis=1, keepdims=True)
-            row = jnp.sum(jnp.where(eye, col, 0.0), axis=0, keepdims=True)
-            sbuf[t, dst + OWN:dst + PC, :] = jnp.zeros((8, D), F32)
-            sbuf[t, dst + OWN:dst + PC, 0:OWN] = jnp.broadcast_to(row, (8, OWN))
+            col = jnp.sum(tacc[slot, j * OWN:(j + 1) * OWN, :], axis=1, keepdims=True)
+            tsend[t * 4 + j] = jnp.sum(jnp.where(wide_eye, col, 0.0), axis=0, keepdims=True)
 
     def chunks(*accumulators):
         scores, moments = accumulators[:NS], accumulators[NS]
@@ -265,12 +277,12 @@
     prows = prow[...]
     pushed_away = inverse_norms(prows) * prows
     cot = jnp.sum(jnp.where(eye, cot_ref[...].reshape(1, OWN), 0.0), axis=1, keepdims=True)
-    own = sbuf[0, 0:PC, :]
+    own, own_totals = sbuf[0, 0:OWN, :], tsend[0]
     for i in range(1, 16):
         to_owner(i // 4, i % 4).wait_recv()
-        own = own + abuf[i]
-    totals = jnp.sum(jnp.where(eye, own[OWN:OWN + 1, 0:OWN], 0.0), axis=1, keepdims=True)
-    pushed = own[0:OWN, :] / totals - pushed_away
+        own, own_totals = own + abuf[i], own_totals + tgot[i]
+    totals = jnp.sum(jnp.where(wide_eye, own_totals, 0.0), axis=1, keepdims=True)
+    pushed = own / totals - pushed_away
     tangent = pushed - dirs * jnp.sum(dirs * pushed, axis=1, keepdims=True)
     gradient = cot * tangent * inv
 
@@ -310,8 +322,10 @@
             pltpu.VMEM((NCH, CH, D), BF16),
             pltpu.VMEM((NW, UNIT, UNIT), BF16),
             pltpu.VMEM((2, CH, 128), F32),
-            pltpu.VMEM((NCH, 4 * PC, D), F32),
-            pltpu.VMEM((16, PC, D), F32),
+            pltpu.VMEM((NCH, CH, D), F32),
+            pltpu.VMEM((16, OWN, D), F32),
+            pltpu.VMEM((16, 1, 128), F32),
+            pltpu.VMEM((16, 1, 128), F32),
             pltpu.VMEM((OWN, D), F32),
             pltpu.VMEM((len(ALL) + 1, 1, 128), F32),
             dma((3,)),
@@ -321,6 +335,7 @@
             dma, dma,
             dma((16,)), dma((16,)),
             dma((16,)), dma((16,)),
+            dma((16,)), dma((16,)),
             dma, dma,
         ],
         compiler_params=pltpu.CompilerParams(

time: 44.5 us -> 44.8 us (level)
  no operation moved by 1% of the time
where the time goes in v7:
time: 44.8 us; the launch traced here: 44.7 us
  Pallas kernels  44 us (98%)
  local copies, waits for them, and re-layouts  0.63 us (1%)
    pallas_call x1, Pallas kernels, shards(): pl.pallas_call(kernel, out_shape=pltpu.VMEM((OWN, D), F32), in_specs=[pl....  44 us

profile of v7, /device:TPU:1, one launch (start us, length us, event | category | flops | bytes accessed | tf_op | source)
XLA Modules:
  0.0 44.7 jit_solution(7106137775394446083)
XLA Ops:
  0.0 44.0 %shard_map.46 = f32[64,256]{1,0:T(8,128)S(1)} custom-call(bf16[64,256]{1,0:T(8,128)(2,1)} %clips_hbm.1, bf16[8192,256]{1,0:T(8,128)(2,1)} %queue_hbm.1, s32[64]{0:T(128)} %pos_hbm.1, f32[64]{0:T(128)} %cot_hbm.1), custom_call_target="tpu_custom_call" | custom-call | flops 16999999488 | bytes 5000000 | tf_op jit(solution)/shard_map/pallas_call | solution.py:311
  44.0 0.6 %copy.6 = f32[64,256]{1,0:T(8,128)} copy(f32[64,256]{1,0:T(8,128)S(1)} %shard_map.46) | data formatting | bytes 131072

commit v8 on v6

--- a/solution.py
+++ b/solution.py
@@ -22,8 +22,8 @@
 NCH = 4
 UNIT = 256
 UNITS = 2 * KQ // UNIT
-LAG_V = 2
-LAG_M = 3
+LAG_V = 3
+LAG_M = 4
 NS = 4
 NW = 4
 QUEUE_WAITS = {32: (0, 1), 44: (2,), 54: (3,)}

time: 44.5 us -> 44.5 us (level)
  no operation moved by 1% of the time
where the time goes in v8:
time: 44.5 us; the launch traced here: 44.4 us
  Pallas kernels  43.7 us (98%)
  local copies, waits for them, and re-layouts  0.63 us (1%)
    pallas_call x1, Pallas kernels, shards(): pl.pallas_call(kernel, out_shape=pltpu.VMEM((OWN, D), F32), in_specs=[pl....  43.7 us

profile of v8, /device:TPU:1, one launch (start us, length us, event | category | flops | bytes accessed | tf_op | source)
XLA Modules:
  0.0 44.4 jit_solution(18395014487388725736)
XLA Ops:
  0.0 43.7 %shard_map.46 = f32[64,256]{1,0:T(8,128)S(1)} custom-call(bf16[64,256]{1,0:T(8,128)(2,1)} %clips_hbm.1, bf16[8192,256]{1,0:T(8,128)(2,1)} %queue_hbm.1, s32[64]{0:T(128)} %pos_hbm.1, f32[64]{0:T(128)} %cot_hbm.1), custom_call_target="tpu_custom_call" | custom-call | flops 16999999488 | bytes 5000000 | tf_op jit(solution)/shard_map/pallas_call | solution.py:299
  43.7 0.6 %copy.6 = f32[64,256]{1,0:T(8,128)} copy(f32[64,256]{1,0:T(8,128)S(1)} %shard_map.46) | data formatting | bytes 131072
